TPU v7x, 768 devices: a whole 4x8x12 slice. The times are simulated.
768 devices in a mesh: grp: 48 (over y, z_lo), tp: 8 (over z_hi, x), role: 2 (over core).
Axes of the slice: x: 4, y: 8, z: 12 (z_hi: 2, z_lo: 6; z = z_hi * 6 + z_lo), core: 2. Of those that a mesh axis runs over, the one named last changes fastest.
Arguments:
- teacher_rows: bfloat16 [12288, 16384], P('grp', ('tp', 'role'))
- teacher_gain: float32 [16384], P(('tp', 'role')), may hold values from 0.1 to 1.9
- block_index: int32 [128, 8], replicated, may hold values from 0 to 31, all different within a row
- block_tiles: bfloat16 [128, 8, 128, 128], P(('tp', 'role')), may hold values from -0.09375 to 0.09375
- student_shard: int32 [12288, 1], P('grp'), may hold values from 0 to 47, as said below
- student_rows: bfloat16 [23040, 4096], P('grp'), as said below
- student_gain: float32 [4096], replicated, may hold values from 0.1 to 1.9
- student_weight: bfloat16 [4096, 4096], P(None, ('tp', 'role')), may hold values from -0.09375 to 0.09375
Outputs:
- weight_grad: bfloat16 [196608, 4096], P('grp', ('tp', 'role'))
Inputs may be any that keep to these rules, and one draw needn't show every extreme that they name: `block_index`: the 8 column blocks named by one row block are distinct. `student_shard`: at most 10 of the 256 tokens of one grp index go to one student shard; some student shards get exactly 10 from every grp index; every shard gets at least one token from every grp index. `student_rows`: row g*480 + s*10 + j holds the student input of the j-th token, in token order, of grp index s that goes to student shard g; rows past that number of tokens are zero.
All inputs are finite; a program needn't handle non-finite values.
Results may differ from a plain program's by a relative error of at most 0.0065.
Values may be sent and summed in bfloat16 or wider, within the bound.
No kernel may reach another device: no remote copies, remote signals or barrier semaphores. Data moves between devices by JAX's collectives and lax.ppermute only.
A program may use at most 64 MiB of HBM per device.

v0:
```python
import math

import jax
import jax.numpy as jnp
from jax import lax
from jax.sharding import PartitionSpec as P

DT = 16384
DS = 4096
TILE = 128


EPS = 1e-05


def tile_products(rows, tiles):
    blocks = rows.reshape(rows.shape[0], tiles.shape[0], tiles.shape[2])
    return jnp.einsum("tbi,bkij->tbkj", blocks, tiles, preferred_element_type=jnp.float32)


def place_columns(products, columns, count):
    wanted = lax.iota(jnp.int32, count)
    select = (columns[:, :, None] == wanted[None, None, :]).astype(jnp.float32)
    return jnp.einsum("tbkj,bkc->ctj", products, select, precision=lax.Precision.HIGHEST)


def on_device(
    teacher_rows,
    teacher_gain,
    block_index,
    block_tiles,
    student_shard,
    student_rows,
    student_gain,
    student_weight,
):
    tokens_here = teacher_rows.shape[0]
    local_blocks = block_tiles.shape[0]
    cores = lax.axis_size("role")
    group = lax.axis_size("tp") * cores
    col_local = DS // TILE // group
    wide = teacher_rows.astype(jnp.float32)
    sums = lax.psum(jnp.sum(wide * wide, axis=1), ("tp", "role"))
    inv_norm = lax.rsqrt(sums / DT + EPS)
    gained = (teacher_rows * teacher_gain).astype(jnp.bfloat16)
    tensor_index = lax.axis_index("tp") * cores + lax.axis_index("role")
    columns = lax.dynamic_slice_in_dim(block_index, tensor_index * local_blocks, local_blocks, 0)
    products = tile_products(gained, block_tiles)
    summed = lax.psum_scatter(
        place_columns(products, columns, lax.axis_size(("tp", "role")) * col_local),
        ("tp", "role"),
        scatter_dimension=0,
        tiled=True,
    )
    targets = (inv_norm[None, :, None] * summed).astype(jnp.bfloat16)
    shards = lax.axis_size("grp")
    capacity = student_rows.shape[0] // shards
    dest = student_shard[:, 0]
    hits = (dest[:, None] == lax.iota(jnp.int32, shards)[None, :]).astype(jnp.int32)
    rank = jnp.sum((jnp.cumsum(hits, axis=0) - hits) * hits, axis=1)
    slot_ids = dest * capacity + rank
    send_matrix = (lax.iota(jnp.int32, shards * capacity)[:, None] == slot_ids[None, :]).astype(
        jnp.bfloat16
    )
    packed = jnp.einsum(
        "st,ctj->scj", send_matrix, targets, preferred_element_type=jnp.float32
    ).astype(jnp.bfloat16)
    packed = packed.reshape(shards, capacity, col_local * TILE)
    received = lax.all_to_all(packed, "grp", split_axis=0, concat_axis=0, tiled=True).reshape(
        shards * capacity, col_local * TILE
    )
    values = student_rows.astype(jnp.float32)
    scale = lax.rsqrt(jnp.mean(values * values, axis=1) + EPS)
    normed = (values * scale[:, None] * student_gain).astype(jnp.bfloat16)
    student_out = jnp.dot(normed, student_weight, preferred_element_type=jnp.float32)
    factor = 1.0 / math.sqrt(tokens_here)
    out_grad = ((student_out - received.astype(jnp.float32)) * factor).astype(jnp.bfloat16)
    weight_grad = lax.dot_general(
        normed, out_grad, (((0,), (0,)), ((), ())), preferred_element_type=jnp.float32
    )
    return weight_grad.astype(jnp.bfloat16)


def solution(mesh):
    placed = (
        P("grp", ("tp", "role")),
        P(("tp", "role")),
        P(),
        P(("tp", "role"), None, None, None),
        P("grp", None),
        P("grp", None),
        P(),
        P(None, ("tp", "role")),
    )
    return jax.shard_map(
        on_device, mesh=mesh, in_specs=placed, out_specs=P("grp", ("tp", "role")), check_vma=False
    )
```

profile of v0, /device:TPU:8, one launch (start us, length us, event | category | flops | bytes accessed | tf_op | source)
XLA Modules:
  0.0 214.4 jit_solution(12818159373017648176)
XLA Ops:
  6.5 0.0 copy-start
  6.5 0.0 reduce-scatter.2.cloned.1.call-start
  6.5 0.9 constant_dynamic-slice_fusion
  7.4 0.1 copy.11
  7.5 1.3 fusion.11
  8.8 0.1 copy.19
  8.9 0.0 copy-done
  8.9 1.2 convolution_bitcast_fusion
  10.2 8.2 %fusion = f32[32,256,128,1]{2,0,3,1:T(8,128)S(1)} fusion(f32[256,8,8,128]{3,0,2,1:T(8,128)S(1)} %convolution_bitcast_fusion, s32[8,8]{1,0:T(8,128)S(1)} %copy.11), kind=kOutput, calls=%fused_computation.2 | convolution fusion | flops 805308416 | bytes 12583168 | tf_op jit(solution)/shard_map/tbkj,bkc->ctj/dot_general | solution.py:24
  18.4 4.5 %copy.26 = f32[32,256,128,1]{2,1,0,3:T(8,128)} copy(f32[32,256,128,1]{2,0,3,1:T(8,128)S(1)} %fusion) | data formatting | bytes 8388608 | tf_op jit(solution)/shard_map/tbkj,bkc->ctj/dot_general | solution.py:24
  22.9 0.0 copy-start.1
  22.9 0.0 reduce-scatter.2.cloned.1.call-update
  22.9 0.0 copy-start.2
  23.0 0.6 copy-done.1
  23.6 0.6 reduce-window.6
  24.2 0.2 slice_reduce_fusion
  24.4 67.5 %psum.7 = f32[256]{0:T(256)S(1)} all-reduce(f32[256]{0:T(256)S(1)} %get-tuple-element.5), channel_id=1, replica_groups=mesh['grp'=48,'tp'=8,'role'=2] {'tp','role'}, use_global_device_ids=true, to_apply=%region_5.6 | all-reduce | flops 256 | bytes 2048 | tf_op jit(solution)/shard_map/psum | solution.py:43
  91.9 0.1 fusion.22
  92.0 76.8 %reduce-scatter.2.cloned.1.call-done = f32[2,256,128]{2,1,0:T(8,128)} async-done(((f32[32,256,128]{2,1,0:T(8,128)}), f32[2,256,128]{2,1,0:T(8,128)}) %reduce-scatter.2.cloned.1.call-update) | async-done | bytes 262160 | tf_op jit(solution)/shard_map/reduce_scatter | solution.py:49
  168.9 1.3 convolution_convert_fusion.1
  170.1 0.2 copy.12
  170.3 0.9 reshape.44
  171.2 8.2 %all-to-all-start = ((bf16[48,10,256]{2,1,0:T(8,128)(2,1)}), bf16[48,10,256]{2,1,0:T(8,128)(2,1)S(1)}, u32[]{:S(2)}, u32[]{:S(2)}) async-start(bf16[48,10,256]{2,1,0:T(8,128)(2,1)} %reshape.44), calls=%async_computation.1 | async-start | bytes 786432 | tf_op jit(solution)/shard_map/all_to_all | solution.py:69
  179.5 3.0 %fusion.2 = f32[480]{0:T(512)S(1)} fusion(bf16[480,4096]{1,0:T(8,128)(2,1)} %param.13), kind=kLoop, calls=%fused_computation.4 | loop fusion | flops 5897760 | bytes 3934080 | tf_op jit(solution)/shard_map/reduce_sum | solution.py:73
  182.4 15.2 %all-to-all-done = bf16[48,10,256]{2,1,0:T(8,128)(2,1)S(1)} async-done(((bf16[48,10,256]{2,1,0:T(8,128)(2,1)}), bf16[48,10,256]{2,1,0:T(8,128)(2,1)S(1)}, u32[]{:S(2)}, u32[]{:S(2)}) %all-to-all-start) | async-done | bytes 245792 | tf_op jit(solution)/shard_map/all_to_all | solution.py:69
  197.7 0.1 reshape.45
  197.7 0.0 copy-done.2
  197.7 9.8 %convolution_convert_fusion = bf16[4096,256]{1,0:T(8,128)(2,1)} fusion(bf16[480,4096]{1,0:T(8,128)(2,1)} %param.13, f32[4096]{0:T(1024)S(1)} %copy-done.2, f32[480]{0:T(512)S(1)} %add_rsqrt_fusion, f32[480,256]{1,0:T(8,128)S(1)} %reshape.45, bf16[4096,256]{1,0:T(8,128)(2,1)} %param.15), kind=kOutput, calls=%fused_computation.7 | convolution fusion | flops 2030411776 | bytes 8636288 | tf_op jit(solution)/shard_map/dot_general | solution.py:78
  (6 shorter events, 0.1 us)
Async XLA Ops:
  6.5 2.4 %copy-start = (bf16[8,8,128,128]{3,2,1,0:T(8,128)(2,1)S(1)}, bf16[8,8,128,128]{3,2,1,0:T(8,128)(2,1)}, u32[]{:S(2)}) copy-start(bf16[8,8,128,128]{3,2,1,0:T(8,128)(2,1)} %param.11) | copy-start | bytes 6291460
  6.5 162.3 %reduce-scatter.2.cloned.1.call-start = ((), (), s32[]{:S(2)}) async-start(), calls=%async_computation.2 | async-start | bytes 4456448 | tf_op jit(solution)/shard_map/reduce_scatter | solution.py:49
  22.9 0.7 copy-start.1
  22.9 174.8 %copy-start.2 = (f32[4096]{0:T(1024)S(1)}, f32[4096]{0:T(1024)}, u32[]{:S(2)}) copy-start(f32[4096]{0:T(1024)} %param.14) | copy-start | bytes 49156
  171.2 26.4 %all-to-all-start = ((bf16[48,10,256]{2,1,0:T(8,128)(2,1)}), bf16[48,10,256]{2,1,0:T(8,128)(2,1)S(1)}, u32[]{:S(2)}, u32[]{:S(2)}) async-start(bf16[48,10,256]{2,1,0:T(8,128)(2,1)} %reshape.44), calls=%async_computation.1 | async-start | bytes 786432 | tf_op jit(solution)/shard_map/all_to_all | solution.py:69
Sparse Core Ops, SparseCore 0:
  23.1 145.7 reduce-scatter.1
where the time goes:
time: 215 us; the launch traced here: 214 us
  waiting for transfers between devices  92.1 us (43%)
  blocking collectives  67.5 us (31%)
  matrix products  20.5 us (10%)
  between operations  13.5 us (6%)
  starting transfers between devices  8.21 us (4%)
  local copies, waits for them, and re-layouts  7.64 us (4%)
  other arithmetic  5 us (2%)
    reduce_scatter x1, waiting for transfers between devices, on_device(): lax.psum_scatter(place_columns(products, columns, lax.axis_size(('tp', 'r...  76.8 us
    psum x1, blocking collectives, on_device(): sums = lax.psum(jnp.sum(wide * wide, axis=1), ('tp', 'role'))  67.5 us
    all_to_all x1, waiting for transfers between devices, on_device(): lax.all_to_all(packed, 'grp', split_axis=0, concat_axis=0, tiled=True)  15.2 us
    dot_general x1, matrix products, on_device(): lax.dot_general(normed, out_grad, (((0,), (0,)), ((), ())), preferred_ele...  9.79 us
    all_to_all x1, starting transfers between devices, on_device(): lax.all_to_all(packed, 'grp', split_axis=0, concat_axis=0, tiled=True)  8.21 us
    dot_general x1, matrix products, place_columns(): jnp.einsum('tbkj,bkc->ctj', products, select, precision=lax.Precision.HIG...  8.21 us
    dot_general x1, local copies, waits for them, and re-layouts, place_columns(): jnp.einsum('tbkj,bkc->ctj', products, select, precision=lax.Precision.HIG...  4.54 us
  transfers between devices with their start and end apart: 2, of which 2 were waited for; matrix products, arithmetic and copies ran while one was open for 2% of the time, Pallas kernels for 0%

commit v1 on v0

v1 whole, which is shorter than its diff:
```python
import math

import jax
import jax.numpy as jnp
from jax import lax
from jax.experimental import pallas as pl
from jax.experimental.pallas import tpu as pltpu
from jax.sharding import PartitionSpec as P

DT = 16384
DS = 4096
TILE = 128
EPS = 1e-05
F32 = jnp.float32
BF16 = jnp.bfloat16
VMEM = pl.BlockSpec(memory_space=pltpu.VMEM)
SMEM = pl.BlockSpec(memory_space=pltpu.SMEM)
TOK = 256
CAP = 10
PAD = 24
TAIL = 16


def params():
    return pltpu.CompilerParams(vmem_limit_bytes=48 * 1024 * 1024)


def pack_sums(row):
    high = row.astype(BF16).astype(F32)
    low = row - high
    return jnp.concatenate([high, low, jnp.zeros((TAIL - 4, TILE), F32)], axis=0).astype(BF16)


def read_sums(tail):
    wide = tail.astype(F32)
    return wide[0:2] + wide[2:4]


def teacher_kernel(index_ref, rows_ref, gain_ref, tiles_ref, send_ref, keep_ref, acc):
    role = lax.axis_index("role")
    base = (lax.axis_index("tp") * 2 + role) * 8
    acc[...] = jnp.zeros_like(acc)
    squares = jnp.zeros((TOK, TILE), F32)
    for b in range(8):
        lanes = slice(b * TILE, (b + 1) * TILE)
        wide = rows_ref[:, lanes].astype(F32)
        squares = squares + wide * wide
        gained = (wide * gain_ref[:, lanes]).astype(BF16)
        tiles = jnp.concatenate([tiles_ref[b, k] for k in range(8)], axis=1)
        products = jnp.dot(gained, tiles, preferred_element_type=F32)
        for k in range(8):
            c = index_ref[k, base + b]
            own = 1 - jnp.bitwise_xor((c >> 1) & 1, role)
            place = own * 16 + ((c >> 2) & 3) * 4 + (c >> 4) * 2 + (c & 1)
            acc[place] += products[:, k * TILE : (k + 1) * TILE]
    for n in range(16):
        send_ref[n * TOK : (n + 1) * TOK, :] = acc[n].astype(BF16)
        keep_ref[n] = acc[16 + n]
    sums = jnp.sum(squares, axis=1, keepdims=True)
    row = jnp.concatenate(
        [
            jnp.transpose(jnp.broadcast_to(sums[h * TILE : (h + 1) * TILE], (TILE, TILE)))[0:1]
            for h in range(2)
        ],
        axis=0,
    )
    send_ref[16 * TOK :, :] = pack_sums(row)


def chip_kernel(send_ref, keep_ref, recv_ref, out_ref):
    tail = pack_sums(read_sums(send_ref[16 * TOK :, :]) + read_sums(recv_ref[16 * TOK :, :]))
    for x in range(4):
        for n in range(4):
            m = x * 4 + n
            out_ref[x, n * TOK : (n + 1) * TOK, :] = (
                keep_ref[m] + recv_ref[m * TOK : (m + 1) * TOK, :].astype(F32)
            ).astype(BF16)
        out_ref[x, 4 * TOK :, :] = tail


def line_kernel(recv_ref, send_ref, keep_ref):
    high = lax.axis_index("tp") // 4
    own = pl.ds(pl.multiple_of(high * 2 * TOK, 2 * TOK), 2 * TOK)
    other = pl.ds(pl.multiple_of((1 - high) * 2 * TOK, 2 * TOK), 2 * TOK)
    tail = slice(4 * TOK, 4 * TOK + TAIL)

    def total(rows):
        wide = [recv_ref[x, rows, :].astype(F32) for x in range(4)]
        return (wide[0] + wide[1]) + (wide[2] + wide[3])

    send_ref[: 2 * TOK, :] = total(other).astype(BF16)
    sums = sum(read_sums(recv_ref[x, tail, :]) for x in range(4))
    send_ref[2 * TOK :, :] = pack_sums(sums)
    keep_ref[...] = total(own)


def pack_kernel(send_ref, keep_ref, recv_ref, slot_ref, out_ref):
    sums = read_sums(send_ref[2 * TOK :, :]) + read_sums(recv_ref[2 * TOK :, :])
    inv = lax.rsqrt(sums / DT + EPS)
    scale = [
        jnp.transpose(jnp.broadcast_to(inv[h : h + 1], (TILE, TILE))) for h in range(2)
    ]
    scale = jnp.concatenate(scale, axis=0)
    rows = slot_ref[0:1, :]
    wanted = lax.broadcasted_iota(jnp.int32, (out_ref.shape[0], TOK), 0)
    packed = jnp.zeros(out_ref.shape, F32)
    for j in range(2):
        part = slice(j * TOK, (j + 1) * TOK)
        targets = (scale * (keep_ref[part, :] + recv_ref[part, :].astype(F32))).astype(BF16)
        place = jnp.where(wanted == rows + j * CAP, 1.0, 0.0).astype(BF16)
        packed = packed + jnp.dot(place, targets, preferred_element_type=F32)
    out_ref[...] = packed.astype(BF16)


def student_kernel(shard_ref, rows_ref, gain_ref, weight_ref, slot_ref, out_ref, turned_ref):
    shards = 48
    dest = shard_ref[...]
    hits = jnp.where(
        lax.broadcasted_iota(jnp.int32, (shards, TOK), 0) == dest, 1.0, 0.0
    )
    earlier = jnp.where(
        lax.broadcasted_iota(jnp.int32, (TOK, TOK), 0)
        < lax.broadcasted_iota(jnp.int32, (TOK, TOK), 1),
        1.0,
        0.0,
    ).astype(BF16)
    counts = jnp.dot(hits.astype(BF16), earlier, preferred_element_type=F32)
    rank = jnp.sum(counts * hits, axis=0, keepdims=True).astype(jnp.int32)
    slot_ref[...] = jnp.broadcast_to(dest * PAD + rank, slot_ref.shape)
    step = 512
    count = rows_ref.shape[0]
    squares = jnp.zeros((count, TILE), F32)
    for n in range(DS // TILE):
        wide = rows_ref[:, n * TILE : (n + 1) * TILE].astype(F32)
        squares = squares + wide * wide
    scale = lax.rsqrt(jnp.sum(squares, axis=1, keepdims=True) / DS + EPS)
    out_ref[...] = jnp.zeros_like(out_ref)
    for n in range(DS // step):
        part = slice(n * step, (n + 1) * step)
        normed = (rows_ref[:, part].astype(F32) * scale * gain_ref[:, part]).astype(BF16)
        out_ref[...] += jnp.dot(normed, weight_ref[part, :], preferred_element_type=F32)
        turned_ref[part, :] = jnp.transpose(normed)


def grad_kernel(recv_ref, out_ref, turned_ref, grad_ref, delta):
    @pl.when(pl.program_id(0) == 0)
    def _():
        count, rows = out_ref.shape[0], recv_ref.shape[0]
        slot = lax.broadcasted_iota(jnp.int32, (count, rows), 0)
        row = lax.broadcasted_iota(jnp.int32, (count, rows), 1)
        place = slot // CAP * PAD + slot % CAP
        for j in range(2):
            lanes = slice(j * TILE, (j + 1) * TILE)
            pick = jnp.where(row == place + j * CAP, 1.0, 0.0).astype(BF16)
            wanted = jnp.dot(pick, recv_ref[...], preferred_element_type=F32)
            delta[:, lanes] = ((out_ref[:, lanes] - wanted) * (1.0 / math.sqrt(TOK))).astype(BF16)

    grad_ref[...] = jnp.dot(
        turned_ref[...], delta[...], preferred_element_type=F32
    ).astype(BF16)


def on_device(
    teacher_rows,
    teacher_gain,
    block_index,
    block_tiles,
    student_shard,
    student_rows,
    student_gain,
    student_weight,
):
    shards = lax.axis_size("grp")
    count = student_rows.shape[0]
    send, keep = pl.pallas_call(
        teacher_kernel,
        out_shape=(
            jax.ShapeDtypeStruct((16 * TOK + TAIL, TILE), BF16),
            jax.ShapeDtypeStruct((16, TOK, TILE), F32),
        ),
        in_specs=[SMEM, VMEM, VMEM, VMEM],
        out_specs=(VMEM, VMEM),
        scratch_shapes=[pltpu.VMEM((32, TOK, TILE), F32)],
        compiler_params=params(),
        cost_estimate=pl.CostEstimate(flops=540000000, bytes_accessed=6000000, transcendentals=0),
        name="teacher",
    )(block_index.T, teacher_rows, teacher_gain[None, :], block_tiles)
    recv = lax.ppermute(send, "role", [(0, 1), (1, 0)])
    student_rows, student_shard, recv = lax.optimization_barrier(
        (student_rows, student_shard, recv)
    )
    line = pl.pallas_call(
        chip_kernel,
        out_shape=jax.ShapeDtypeStruct((4, 4 * TOK + TAIL, TILE), BF16),
        in_specs=[VMEM] * 3,
        out_specs=VMEM,
        compiler_params=params(),
        cost_estimate=pl.CostEstimate(flops=1000000, bytes_accessed=4000000, transcendentals=0),
        name="chip",
    )(send, keep, recv)
    groups = [[z * 4 + x for x in range(4)] for z in range(2)]
    line = lax.all_to_all(line, "tp", 0, 0, tiled=True, axis_index_groups=groups)
    slots, student_out, turned = pl.pallas_call(
        student_kernel,
        out_shape=(
            jax.ShapeDtypeStruct((8, TOK), jnp.int32),
            jax.ShapeDtypeStruct((count, 2 * TILE), F32),
            jax.ShapeDtypeStruct((DS, count), BF16),
        ),
        in_specs=[VMEM] * 4,
        out_specs=(VMEM,) * 3,
        compiler_params=params(),
        cost_estimate=pl.CostEstimate(flops=2000000000, bytes_accessed=10000000, transcendentals=480),
        name="student",
    )(student_shard.reshape(1, TOK), student_rows, student_gain[None, :], student_weight)
    half, own = pl.pallas_call(
        line_kernel,
        out_shape=(
            jax.ShapeDtypeStruct((2 * TOK + TAIL, TILE), BF16),
            jax.ShapeDtypeStruct((2 * TOK, TILE), F32),
        ),
        in_specs=[VMEM],
        out_specs=(VMEM, VMEM),
        compiler_params=params(),
        cost_estimate=pl.CostEstimate(flops=1000000, bytes_accessed=2000000, transcendentals=0),
        name="line",
    )(line)
    far = lax.ppermute(half, "tp", [(n, (n + 4) % 8) for n in range(8)])
    packed = pl.pallas_call(
        pack_kernel,
        out_shape=jax.ShapeDtypeStruct((shards * PAD, TILE), BF16),
        in_specs=[VMEM] * 4,
        out_specs=VMEM,
        compiler_params=params(),
        cost_estimate=pl.CostEstimate(flops=150000000, bytes_accessed=1000000, transcendentals=256),
        name="pack",
    )(half, own, far, slots)
    arrived = lax.all_to_all(
        packed.reshape(shards, PAD, TILE), "grp", split_axis=0, concat_axis=0, tiled=True
    )
    block = 1024
    return pl.pallas_call(
        grad_kernel,
        grid=(DS // block,),
        out_shape=jax.ShapeDtypeStruct((DS, 2 * TILE), BF16),
        in_specs=[
            pl.BlockSpec((shards * PAD, TILE), lambda i: (0, 0)),
            pl.BlockSpec((count, 2 * TILE), lambda i: (0, 0)),
            pl.BlockSpec((block, count), lambda i: (i, 0)),
        ],
        out_specs=pl.BlockSpec((block, 2 * TILE), lambda i: (i, 0)),
        scratch_shapes=[pltpu.VMEM((count, 2 * TILE), BF16)],
        compiler_params=params(),
        cost_estimate=pl.CostEstimate(flops=1000000000, bytes_accessed=7000000, transcendentals=0),
        name="grad",
    )(arrived.reshape(shards * PAD, TILE), student_out, turned)


def solution(mesh):
    placed = (
        P("grp", ("tp", "role")),
        P(("tp", "role")),
        P(),
        P(("tp", "role"), None, None, None),
        P("grp", None),
        P("grp", None),
        P(),
        P(None, ("tp", "role")),
    )
    return jax.shard_map(
        on_device, mesh=mesh, in_specs=placed, out_specs=P("grp", ("tp", "role")), check_vma=False
    )
```

time: 215 us -> 91 us (0.42)
  waiting for transfers between devices: 92.1 us -> 3.77 us
  matrix products: 20.5 us -> 0 us
  blocking collectives: 67.5 us -> 50.1 us
  between operations: 13.5 us -> 0.09 us
  Pallas kernels: 0 us -> 13.4 us
  starting transfers between devices: 8.21 us -> 17.1 us
  other arithmetic: 5 us -> 0 us
    reduce_scatter x1 -> x0, waiting for transfers between devices: 76.8 us -> none  [on_device(): lax.psum_scatter(place_columns(products, columns, lax.axis_size(('tp', 'r...]
    psum x1 -> x0, blocking collectives: 67.5 us -> none  [on_device(): sums = lax.psum(jnp.sum(wide * wide, axis=1), ('tp', 'role'))]
    all_to_all x0 -> x2, blocking collectives: none -> 50.1 us  [the longest x1 30.3 us: on_device(): lax.all_to_all(packed.reshape(shards, PAD, TILE), 'grp', split_axis=0, co...]
    dot_general x4 -> x0, matrix products: 20.5 us -> none  [the longest x1 9.79 us: on_device(): lax.dot_general(normed, out_grad, (((0,), (0,)), ((), ())), preferred_ele...]
    ppermute x0 -> x2, starting transfers between devices: none -> 17.1 us  [the longest x1 15.1 us: on_device(): far = lax.ppermute(half, 'tp', [(n, (n + 4) % 8) for n in range(8)])]
    all_to_all x1 -> x0, waiting for transfers between devices: 15.2 us -> none  [on_device(): lax.all_to_all(packed, 'grp', split_axis=0, concat_axis=0, tiled=True)]
    pallas_call x0 -> x6, Pallas kernels: none -> 13.4 us  [the longest x1 6.22 us: on_device(): pl.pallas_call(student_kernel, out_shape=(jax.ShapeDtypeStruct((8, TOK),...]
    all_to_all x1 -> x0, starting transfers between devices: 8.21 us -> none  [on_device(): lax.all_to_all(packed, 'grp', split_axis=0, concat_axis=0, tiled=True)]
  transfers between devices with their start and end apart: 2 -> 2, of which waited for: 2 -> 2; matrix products, arithmetic and copies ran while one was open for 2% -> 0% of each run, Pallas kernels for 0% -> 7%
where the time goes in v1:
time: 91 us; the launch traced here: 90.6 us
  blocking collectives  50.1 us (55%)
  starting transfers between devices  17.1 us (19%)
  Pallas kernels  13.4 us (15%)
  local copies, waits for them, and re-layouts  6.21 us (7%)
  waiting for transfers between devices  3.77 us (4%)
    all_to_all x1, blocking collectives, on_device(): lax.all_to_all(packed.reshape(shards, PAD, TILE), 'grp', split_axis=0, co...  30.3 us
    all_to_all x1, blocking collectives, on_device(): lax.all_to_all(line, 'tp', 0, 0, tiled=True, axis_index_groups=groups)  19.8 us
    ppermute x1, starting transfers between devices, on_device(): far = lax.ppermute(half, 'tp', [(n, (n + 4) % 8) for n in range(8)])  15.1 us
    pallas_call x1, Pallas kernels, on_device(): pl.pallas_call(student_kernel, out_shape=(jax.ShapeDtypeStruct((8, TOK),...  6.22 us
    unnamed x16, local copies, waits for them, and re-layouts  6.21 us
    pallas_call x1, Pallas kernels, on_device(): pl.pallas_call(grad_kernel, grid=(DS // block,), out_shape=jax.ShapeDtype...  3.66 us
    ppermute x1, waiting for transfers between devices, on_device(): recv = lax.ppermute(send, 'role', [(0, 1), (1, 0)])  2.63 us
    pallas_call x1, Pallas kernels, on_device(): pl.pallas_call(teacher_kernel, out_shape=(jax.ShapeDtypeStruct((16 * TOK...  2.52 us
  transfers between devices with their start and end apart: 2, of which 2 were waited for; matrix products, arithmetic and copies ran while one was open for 0% of the time, Pallas kernels for 7%

profile of v1, /device:TPU:8, one launch (start us, length us, event | category | flops | bytes accessed | tf_op | source)
XLA Modules:
  0.0 90.6 jit_solution(14530190565337075116)
XLA Ops:
  0.0 0.0 copy-start.1
  0.0 1.6 %copy-done.1 = bf16[8,8,128,128]{3,2,1,0:T(8,128)(2,1)S(1)} copy-done((bf16[8,8,128,128]{3,2,1,0:T(8,128)(2,1)S(1)}, bf16[8,8,128,128]{3,2,1,0:T(8,128)(2,1)}, u32[]{:S(2)}) %copy-start.1) | copy-done | bytes 2097176
  1.6 0.0 copy-start.2
  1.6 1.0 %copy-done.2 = bf16[256,1024]{1,0:T(8,128)(2,1)S(1)} copy-done((bf16[256,1024]{1,0:T(8,128)(2,1)S(1)}, bf16[256,1024]{1,0:T(8,128)(2,1)}, u32[]{:S(2)}) %copy-start.2) | copy-done | bytes 524312
  2.6 0.0 copy-start.3
  2.6 0.7 copy-done.3
  3.3 0.0 copy-start.4
  3.3 0.7 copy-done.4
  4.0 2.5 %teacher.1 = (bf16[4112,128]{1,0:T(8,128)(2,1)S(1)}, f32[16,256,128]{2,1,0:T(8,128)S(1)}) custom-call(s32[8,128]{1,0:T(8,128)S(1)} %bitcast.8, bf16[256,1024]{1,0:T(8,128)(2,1)S(1)} %copy-done.2, f32[1,1024]{1,0:T(1,128)S(1)} %bitcast.9, bf16[8,8,128,128]{3,2,1,0:T(8,128)(2,1)S(1)} %copy-done.1), custom_call_target="tpu_custom_call" | custom-call | flops 540000000 | bytes 6000000 | tf_op jit(solution)/shard_map/teacher/pallas_call | solution.py:175
  6.5 1.9 %collective-permute-start = (bf16[4112,128]{1,0:T(8,128)(2,1)S(1)}, bf16[4112,128]{1,0:T(8,128)(2,1)S(1)}, u32[]{:S(2)}, u32[]{:S(2)}) collective-permute-start(bf16[4112,128]{1,0:T(8,128)(2,1)S(1)} %get-tuple-element.15.send_ref), channel_id=1, source_target_pairs={{0,1},{1,0},{2,3},{3,2},{4,5},{5,4},{6,7},{7,6},{8,9},{9,8},{10,11... | collective-permute-start | bytes 3158024 | tf_op jit(solution)/shard_map/ppermute | solution.py:188
  8.5 2.6 %collective-permute-done.recv_ref = bf16[4112,128]{1,0:T(8,128)(2,1)S(1)} collective-permute-done((bf16[4112,128]{1,0:T(8,128)(2,1)S(1)}, bf16[4112,128]{1,0:T(8,128)(2,1)S(1)}, u32[]{:S(2)}, u32[]{:S(2)}) %collective-permute-start) | collective-permute-done | bytes 1052704 | tf_op jit(solution)/shard_map/ppermute | solution.py:188
  11.1 0.3 chip.1
  11.4 0.0 copy-start.5
  11.4 0.0 copy-start.6
  11.4 0.0 copy-start.7
  11.4 19.8 %all_to_all.10.recv_ref = bf16[4,1040,128]{2,1,0:T(8,128)(2,1)S(1)} all-to-all(bf16[4,1040,128]{2,1,0:T(8,128)(2,1)S(1)} %chip.1), channel_id=1, replica_groups={{0,2,4,6},{8,10,12,14},{1,3,5,7},{9,11,13,15},{16,18,20,22},{24,26,28,3..., dimensions={0} | all-to-all | bytes 2129920 | tf_op jit(solution)/shard_map/all_to_all | solution.py:202
  31.2 0.1 line.1
  31.4 15.1 %collective-permute-start.1 = (bf16[528,128]{1,0:T(8,128)(2,1)S(1)}, bf16[528,128]{1,0:T(8,128)(2,1)S(1)}, u32[]{:S(2)}, u32[]{:S(2)}) collective-permute-start(bf16[528,128]{1,0:T(8,128)(2,1)S(1)} %get-tuple-element.18.send_ref), channel_id=1, source_target_pairs={{0,8},{2,10},{4,12},{6,14},{8,0},{10,2},{12,4},{14,6},{1,9},{3,11}... | collective-permute-start | bytes 405512 | tf_op jit(solution)/shard_map/ppermute | solution.py:228
  46.5 0.0 copy-done.5
  46.5 0.0 copy-done.6
  46.5 0.0 copy-done.7
  46.5 6.2 %student.1 = (s32[8,256]{1,0:T(8,128)S(1)}, f32[480,256]{1,0:T(8,128)S(1)}, bf16[4096,480]{1,0:T(8,128)(2,1)}) custom-call(s32[1,256]{1,0:T(1,128)S(1)} %bitcast.11, bf16[480,4096]{1,0:T(8,128)(2,1)} %rows_ref.2, f32[1,4096]{1,0:T(1,128)S(1)} %bitcast.10, bf16[4096,256]{1,0:T(8,128)(2,1)S(1)} %copy-done.5), custom_call_target="tpu_custom_call" | custom-call | flops 2000000000 | bytes 10000000 | tf_op jit(solution)/shard_map/student/pallas_call | solution.py:203
  52.8 1.1 %collective-permute-done.1.recv_ref = bf16[528,128]{1,0:T(8,128)(2,1)S(1)} collective-permute-done((bf16[528,128]{1,0:T(8,128)(2,1)S(1)}, bf16[528,128]{1,0:T(8,128)(2,1)S(1)}, u32[]{:S(2)}, u32[]{:S(2)}) %collective-permute-start.1) | collective-permute-done | bytes 135200 | tf_op jit(solution)/shard_map/ppermute | solution.py:228
  53.9 0.6 pack.1
  54.5 30.3 %all_to_all.11 = bf16[48,24,128]{2,1,0:T(8,128)(2,1)S(1)} all-to-all(bf16[48,24,128]{2,1,0:T(8,128)(2,1)S(1)} %bitcast.7), channel_id=1, replica_groups=mesh['grp'=48,'tp'=8,'role'=2] {'grp'}, dimensions={0} | all-to-all | bytes 589824 | tf_op jit(solution)/shard_map/all_to_all | solution.py:238
  84.7 0.0 copy-start
  84.8 2.2 %copy-done = bf16[4096,480]{1,0:T(8,128)(2,1)S(1)} copy-done((bf16[4096,480]{1,0:T(8,128)(2,1)S(1)}, bf16[4096,480]{1,0:T(8,128)(2,1)}, u32[]{:S(2)}) %copy-start) | copy-done | bytes 3932184
  86.9 3.7 %grad.1 = bf16[4096,256]{1,0:T(8,128)(2,1)} custom-call(bf16[1152,128]{1,0:T(8,128)(2,1)S(1)} %bitcast.6, f32[480,256]{1,0:T(8,128)S(1)} %get-tuple-element.23.out_ref, bf16[4096,480]{1,0:T(8,128)(2,1)S(1)} %copy-done), custom_call_target="tpu_custom_call" | custom-call | flops 1000000000 | bytes 7000000 | tf_op jit(solution)/shard_map/grad/pallas_call | solution.py:242
Async XLA Ops:
  0.0 1.6 %copy-start.1 = (bf16[8,8,128,128]{3,2,1,0:T(8,128)(2,1)S(1)}, bf16[8,8,128,128]{3,2,1,0:T(8,128)(2,1)}, u32[]{:S(2)}) copy-start(bf16[8,8,128,128]{3,2,1,0:T(8,128)(2,1)} %tiles_ref.1) | copy-start | bytes 6291460
  1.6 1.0 %copy-start.2 = (bf16[256,1024]{1,0:T(8,128)(2,1)S(1)}, bf16[256,1024]{1,0:T(8,128)(2,1)}, u32[]{:S(2)}) copy-start(bf16[256,1024]{1,0:T(8,128)(2,1)} %rows_ref.1) | copy-start | bytes 1572868
  2.6 0.7 copy-start.3
  3.3 0.7 copy-start.4
  6.5 4.6 %collective-permute-start = (bf16[4112,128]{1,0:T(8,128)(2,1)S(1)}, bf16[4112,128]{1,0:T(8,128)(2,1)S(1)}, u32[]{:S(2)}, u32[]{:S(2)}) collective-permute-start(bf16[4112,128]{1,0:T(8,128)(2,1)S(1)} %get-tuple-element.15.send_ref), channel_id=1, source_target_pairs={{0,1},{1,0},{2,3},{3,2},{4,5},{5,4},{6,7},{7,6},{8,9},{9,8},{10,11... | collective-permute-start | bytes 3158024 | tf_op jit(solution)/shard_map/ppermute | solution.py:188
  11.4 35.1 %copy-start.5 = (bf16[4096,256]{1,0:T(8,128)(2,1)S(1)}, bf16[4096,256]{1,0:T(8,128)(2,1)}, u32[]{:S(2)}) copy-start(bf16[4096,256]{1,0:T(8,128)(2,1)} %weight_ref.1) | copy-start | bytes 6291460
  11.4 35.1 %copy-start.6 = (f32[4096]{0:T(1024)S(1)}, f32[4096]{0:T(1024)}, u32[]{:S(2)}) copy-start(f32[4096]{0:T(1024)} %param.14) | copy-start | bytes 49156
  11.4 35.1 %copy-start.7 = (s32[256,1]{0,1:T(1,128)S(1)}, s32[256,1]{0,1:T(1,128)}, u32[]{:S(2)}) copy-start(s32[256,1]{0,1:T(1,128)} %param.12) | copy-start | bytes 3076
  31.4 22.5 %collective-permute-start.1 = (bf16[528,128]{1,0:T(8,128)(2,1)S(1)}, bf16[528,128]{1,0:T(8,128)(2,1)S(1)}, u32[]{:S(2)}, u32[]{:S(2)}) collective-permute-start(bf16[528,128]{1,0:T(8,128)(2,1)S(1)} %get-tuple-element.18.send_ref), channel_id=1, source_target_pairs={{0,8},{2,10},{4,12},{6,14},{8,0},{10,2},{12,4},{14,6},{1,9},{3,11}... | collective-permute-start | bytes 405512 | tf_op jit(solution)/shard_map/ppermute | solution.py:228
  84.7 2.2 %copy-start = (bf16[4096,480]{1,0:T(8,128)(2,1)S(1)}, bf16[4096,480]{1,0:T(8,128)(2,1)}, u32[]{:S(2)}) copy-start(bf16[4096,480]{1,0:T(8,128)(2,1)} %get-tuple-element.24.turned_ref) | copy-start | bytes 11796484

commit v2 on v1

v2 whole, which is shorter than its diff:
```python
import math

import jax
import jax.numpy as jnp
from jax import lax
from jax.experimental import pallas as pl
from jax.experimental.pallas import tpu as pltpu
from jax.sharding import PartitionSpec as P

DT = 16384
DS = 4096
TILE = 128
EPS = 1e-05
F32 = jnp.float32
BF16 = jnp.bfloat16
VMEM = pl.BlockSpec(memory_space=pltpu.VMEM)
HBM = pl.BlockSpec(memory_space=pltpu.HBM)
TOK = 256
CAP = 10
PAD = 22
TEACHER_MIB = 58
ROUTE_MIB = 46
STASH = 144
TAIL = 16


def params(mib=24):
    return pltpu.CompilerParams(vmem_limit_bytes=mib * 1024 * 1024)


def pack_sums(row):
    high = row.astype(BF16).astype(F32)
    low = row - high
    return jnp.concatenate([high, low, jnp.zeros((TAIL - 4, TILE), F32)], axis=0).astype(BF16)


def read_sums(tail):
    wide = tail.astype(F32)
    return wide[0:2] + wide[2:4]


def teacher_kernel(
    index_hbm, rows_hbm, gain_hbm, tiles_hbm, send_hbm, keep_hbm,
    index, rows, gain, tiles, acc, send, own_sums, sems
):
    first = [
        pltpu.make_async_copy(rows_hbm, rows, sems.at[8]),
        pltpu.make_async_copy(gain_hbm, gain, sems.at[9]),
        pltpu.make_async_copy(index_hbm, index, sems.at[10]),
    ]
    loads = [pltpu.make_async_copy(tiles_hbm.at[b], tiles.at[b], sems.at[b]) for b in range(8)]
    for copy in first + loads:
        copy.start()
    role = lax.axis_index("role")
    base = (lax.axis_index("tp") * 2 + role) * 8
    acc[...] = jnp.zeros_like(acc)
    squares = jnp.zeros((TOK, TILE), F32)
    for copy in first:
        copy.wait()
    for b in range(8):
        lanes = slice(b * TILE, (b + 1) * TILE)
        wide = rows[:, lanes].astype(F32)
        squares = squares + wide * wide
        gained = (wide * gain[:, lanes]).astype(BF16)
        loads[b].wait()
        side = jnp.concatenate([tiles[b, k] for k in range(8)], axis=1)
        products = jnp.dot(gained, side, preferred_element_type=F32)
        for k in range(8):
            c = index[k, base + b]
            own = 1 - jnp.bitwise_xor((c >> 1) & 1, role)
            place = own * 16 + ((c >> 2) & 3) * 4 + (c >> 4) * 2 + (c & 1)
            acc[place] += products[:, k * TILE : (k + 1) * TILE]
    stores = [
        pltpu.make_async_copy(acc.at[pl.ds(16, 16)], keep_hbm.at[pl.ds(0, 16)], sems.at[11])
    ]
    stores[0].start()
    sums = jnp.sum(squares, axis=1, keepdims=True) * (1.0 / DT)
    row = jnp.concatenate(
        [
            jnp.transpose(jnp.broadcast_to(sums[h * TILE : (h + 1) * TILE], (TILE, TILE)))[0:1]
            for h in range(2)
        ],
        axis=0,
    )
    own_sums[...] = jnp.concatenate([row, jnp.zeros((TAIL - 2, TILE), F32)], axis=0)
    stores.append(
        pltpu.make_async_copy(own_sums, keep_hbm.at[16, pl.ds(0, TAIL)], sems.at[16])
    )
    stores[1].start()
    send[16 * TOK :, :] = pack_sums(row)
    step = 4 * TOK
    for m in range(4):
        for n in range(4 * m, 4 * m + 4):
            send[n * TOK : (n + 1) * TOK, :] = acc[n].astype(BF16)
        here = pl.ds(m * step, step + (TAIL if m == 3 else 0))
        stores.append(pltpu.make_async_copy(send.at[here], send_hbm.at[here], sems.at[12 + m]))
        stores[-1].start()
    for copy in stores:
        copy.wait()


def chip_kernel(tail_ref, keep_ref, recv_ref, out_ref):
    tail = pack_sums(tail_ref[0:2] + read_sums(recv_ref[16 * TOK :, :]))
    for x in range(4):
        for n in range(4):
            m = x * 4 + n
            out_ref[x, n * TOK : (n + 1) * TOK, :] = (
                keep_ref[m] + recv_ref[m * TOK : (m + 1) * TOK, :].astype(F32)
            ).astype(BF16)
        out_ref[x, 4 * TOK :, :] = tail


def route_kernel(
    shard_ref, keep_hbm, place_ref, rank_ref, hits_ref, tail_ref, keep_ref, sems
):
    copies = [
        pltpu.make_async_copy(keep_hbm.at[pl.ds(0, 16)], keep_ref, sems.at[0]),
        pltpu.make_async_copy(keep_hbm.at[16, pl.ds(0, TAIL)], tail_ref, sems.at[1]),
    ]
    for copy in copies:
        copy.start()
    dest = shard_ref[...]
    hits = jnp.where(lax.broadcasted_iota(jnp.int32, hits_ref.shape, 0) == dest, 1.0, 0.0)
    hits_ref[...] = hits.astype(BF16)
    earlier = jnp.where(
        lax.broadcasted_iota(jnp.int32, (TOK, TOK), 0)
        < lax.broadcasted_iota(jnp.int32, (TOK, TOK), 1),
        1.0,
        0.0,
    ).astype(BF16)
    counts = jnp.dot(hits.astype(BF16), earlier, preferred_element_type=F32)
    rank = jnp.sum(counts * hits, axis=0, keepdims=True).astype(jnp.int32)
    rank_ref[...] = jnp.broadcast_to(rank, rank_ref.shape)
    row = lax.broadcasted_iota(jnp.int32, (place_ref.shape[0], TOK), 0)
    for j in range(2):
        wanted = dest * PAD + 2 * rank + j
        place_ref[:, j * TOK : (j + 1) * TOK] = jnp.where(row == wanted, 1.0, 0.0).astype(BF16)
    for copy in copies:
        copy.wait()


def pack_kernel(recv_ref, place_ref, rank_ref, hits_ref, out_hbm, wide, out, sems):
    tail = slice(4 * TOK, 4 * TOK + TAIL)

    def total(n):
        part = [recv_ref[x, n * TOK : (n + 1) * TOK, :].astype(F32) for x in range(4)]
        return ((part[0] + part[1]) + (part[2] + part[3])).astype(BF16)

    sums = sum(read_sums(recv_ref[x, tail, :]) for x in range(4))
    sums = jnp.concatenate([sums[0:1], sums[1:2]], axis=1)
    high = sums.astype(BF16).astype(F32)
    slot = lax.broadcasted_iota(jnp.int32, (TILE, TOK), 0) == rank_ref[0:1, :]
    rows = place_ref.shape[0]
    parts = jnp.concatenate(
        [jnp.concatenate([total(z * 2 + j) for z in range(2)], axis=1) for j in range(2)], axis=0
    )
    moved = jnp.dot(place_ref[...], parts, preferred_element_type=F32)
    for z in range(2):
        wide[z * rows : (z + 1) * rows, :] = moved[:, z * TILE : (z + 1) * TILE]
    for n, values in enumerate((high, sums - high)):
        held = jnp.where(slot, values, 0.0).astype(BF16)
        shown = lax.dot_general(
            hits_ref[...], held, (((1,), (1,)), ((), ())), preferred_element_type=F32
        )
        for z in range(2):
            wide[pl.ds(z * rows + 2 * CAP + n, shown.shape[0], stride=PAD), :] = shown
    copies = []
    for z in range(2):
        here = pl.ds(z * rows, rows)
        out[here, :] = wide[here, :].astype(BF16)
        copies.append(pltpu.make_async_copy(out.at[here], out_hbm.at[here], sems.at[z]))
        copies[z].start()
    for copy in copies:
        copy.wait()


def student_kernel(
    rows_ref, gain_ref, weight_ref, out_ref, stash_hbm, pick_ref, spread_ref, turned_ref, sems
):
    step = DS // 8
    count = rows_ref.shape[0]
    slots = PAD // 2
    squares = jnp.zeros((count, TILE), F32)
    for n in range(DS // TILE):
        wide = rows_ref[:, n * TILE : (n + 1) * TILE].astype(F32)
        squares = squares + wide * wide
    scale = lax.rsqrt(jnp.sum(squares, axis=1, keepdims=True) / DS + EPS)
    out_ref[...] = jnp.zeros_like(out_ref)
    copies = []
    for n in range(DS // step):
        part = slice(n * step, (n + 1) * step)
        normed = (rows_ref[:, part].astype(F32) * scale * gain_ref[:, part]).astype(BF16)
        out_ref[...] += jnp.dot(normed, weight_ref[part, :], preferred_element_type=F32)
        turned_ref[part, :] = jnp.transpose(normed)
        here = pl.ds(n * step, step)
        copies.append(
            pltpu.make_async_copy(turned_ref.at[here], stash_hbm.at[here], sems.at[n])
        )
        copies[n].start()
    wanted = lax.broadcasted_iota(jnp.int32, (count, 1), 0)
    wanted = wanted + wanted // CAP
    pick_ref[...] = jnp.where(
        lax.broadcasted_iota(jnp.int32, pick_ref.shape, 1) == wanted, 1.0, 0.0
    ).astype(BF16)
    source = lax.broadcasted_iota(jnp.int32, (spread_ref.shape[0], 1), 0) // slots
    spread_ref[...] = jnp.where(
        lax.broadcasted_iota(jnp.int32, spread_ref.shape, 1) == source, 1.0, 0.0
    ).astype(BF16)
    for copy in copies:
        copy.wait()


def grad_kernel(
    recv_ref, out_ref, pick_ref, spread_ref, stash_hbm, grad_hbm, wide, turned, grad, sems
):
    steps = sems.shape[1]
    block = DS // steps
    here = [pl.ds(n * block, block) for n in range(steps)]
    loads = [
        pltpu.make_async_copy(stash_hbm.at[here[n]], turned.at[here[n]], sems.at[0, n])
        for n in range(steps)
    ]
    stores = [
        pltpu.make_async_copy(grad.at[here[n]], grad_hbm.at[here[n]], sems.at[1, n])
        for n in range(steps)
    ]
    for copy in loads:
        copy.start()
    slots = PAD // 2
    half = wide.shape[0] // 2
    count = half // 2
    shards = half // PAD
    wide[...] = recv_ref[...].astype(F32)

    def every(start, size, stride):
        return sum(wide[pl.ds(z * half + start, size, stride=stride), :] for z in range(2))

    sums = every(2 * CAP, shards, PAD) + every(2 * CAP + 1, shards, PAD)
    inv = lax.rsqrt(sums + EPS)
    high = inv.astype(BF16)
    low = (inv - high.astype(F32)).astype(BF16)
    rows = jnp.dot(
        spread_ref[...], jnp.concatenate([high, low], axis=1), preferred_element_type=F32
    )
    slot = lax.broadcasted_iota(jnp.int32, (count, 1), 0) % slots
    own = lax.broadcasted_iota(jnp.int32, (count, TILE), 1) == slot
    scale = jnp.sum(jnp.where(own, rows[:, :TILE] + rows[:, TILE:], 0.0), axis=1, keepdims=True)
    targets = jnp.concatenate(
        [(scale * every(j, count, 2)).astype(BF16) for j in range(2)], axis=1
    )
    wanted = jnp.dot(pick_ref[...], targets, preferred_element_type=F32)
    delta = ((out_ref[...] - wanted) * (1.0 / math.sqrt(TOK))).astype(BF16)
    for n in range(steps):
        loads[n].wait()
        grad[here[n], :] = jnp.dot(
            turned[here[n], :], delta, preferred_element_type=F32
        ).astype(BF16)
        stores[n].start()
    for copy in stores:
        copy.wait()


def on_device(
    teacher_rows,
    teacher_gain,
    block_index,
    block_tiles,
    student_shard,
    student_rows,
    student_gain,
    student_weight,
):
    shards = lax.axis_size("grp")
    count = student_rows.shape[0]
    send, keep = pl.pallas_call(
        teacher_kernel,
        out_shape=(
            jax.ShapeDtypeStruct((16 * TOK + TAIL, TILE), BF16),
            jax.ShapeDtypeStruct((STASH, TOK, TILE), F32),
        ),
        in_specs=[HBM] * 4,
        out_specs=(HBM, HBM),
        scratch_shapes=[
            pltpu.SMEM((8, TILE), jnp.int32),
            pltpu.VMEM(teacher_rows.shape, BF16),
            pltpu.VMEM((1, teacher_rows.shape[1]), F32),
            pltpu.VMEM(block_tiles.shape, BF16),
            pltpu.VMEM((32, TOK, TILE), F32),
            pltpu.VMEM((16 * TOK + TAIL, TILE), BF16),
            pltpu.VMEM((TAIL, TILE), F32),
            pltpu.SemaphoreType.DMA((17,)),
        ],
        compiler_params=params(TEACHER_MIB),
        cost_estimate=pl.CostEstimate(flops=540000000, bytes_accessed=6000000, transcendentals=0),
        name="teacher",
    )(block_index.T, teacher_rows, teacher_gain[None, :], block_tiles)
    recv = lax.ppermute(send, "role", [(0, 1), (1, 0)])
    student_shard, keep = lax.optimization_barrier((student_shard, keep))
    place, rank, hits, tail, keep = pl.pallas_call(
        route_kernel,
        out_shape=(
            jax.ShapeDtypeStruct((shards * PAD, 2 * TOK), BF16),
            jax.ShapeDtypeStruct((8, TOK), jnp.int32),
            jax.ShapeDtypeStruct((shards, TOK), BF16),
            jax.ShapeDtypeStruct((TAIL, TILE), F32),
            jax.ShapeDtypeStruct((16, TOK, TILE), F32),
        ),
        in_specs=[VMEM, HBM],
        out_specs=(VMEM,) * 5,
        scratch_shapes=[pltpu.SemaphoreType.DMA((2,))],
        compiler_params=params(ROUTE_MIB),
        cost_estimate=pl.CostEstimate(flops=100000000, bytes_accessed=4000000, transcendentals=0),
        name="route",
    )(student_shard.reshape(1, TOK), keep)
    place, rank, hits, tail, keep, recv = lax.optimization_barrier(
        (place, rank, hits, tail, keep, recv)
    )
    line = pl.pallas_call(
        chip_kernel,
        out_shape=jax.ShapeDtypeStruct((4, 4 * TOK + TAIL, TILE), BF16),
        in_specs=[VMEM] * 3,
        out_specs=VMEM,
        compiler_params=params(),
        cost_estimate=pl.CostEstimate(flops=1000000, bytes_accessed=4000000, transcendentals=0),
        name="chip",
    )(tail, keep, recv)
    groups = [[z * 4 + x for x in range(4)] for z in range(2)]
    line = lax.all_to_all(line, "tp", 0, 0, tiled=True, axis_index_groups=groups)
    packed = pl.pallas_call(
        pack_kernel,
        out_shape=jax.ShapeDtypeStruct((2 * shards * PAD, TILE), BF16),
        in_specs=[VMEM] * 4,
        out_specs=HBM,
        scratch_shapes=[
            pltpu.VMEM((2 * shards * PAD, TILE), F32),
            pltpu.VMEM((2 * shards * PAD, TILE), BF16),
            pltpu.SemaphoreType.DMA((2,)),
        ],
        compiler_params=params(),
        cost_estimate=pl.CostEstimate(flops=400000000, bytes_accessed=2000000, transcendentals=0),
        name="pack",
    )(line, place, rank, hits)
    student_rows, packed = lax.optimization_barrier((student_rows, packed))
    student_out, stash, pick, spread = pl.pallas_call(
        student_kernel,
        out_shape=(
            jax.ShapeDtypeStruct((count, 2 * TILE), F32),
            jax.ShapeDtypeStruct((4 * DS, count), BF16),
            jax.ShapeDtypeStruct((count, shards * PAD // 2), BF16),
            jax.ShapeDtypeStruct((shards * PAD // 2, shards), BF16),
        ),
        in_specs=[VMEM] * 3,
        out_specs=(VMEM, HBM, VMEM, VMEM),
        scratch_shapes=[pltpu.VMEM((DS, count), BF16), pltpu.SemaphoreType.DMA((8,))],
        compiler_params=params(52),
        cost_estimate=pl.CostEstimate(flops=2000000000, bytes_accessed=10000000, transcendentals=480),
        name="student",
    )(student_rows, student_gain[None, :], student_weight)
    groups = [
        [(g * 8 + z * 4 + x) * 2 + c for z in range(2) for g in range(shards)]
        for x in range(4)
        for c in range(2)
    ]
    arrived = lax.all_to_all(
        packed.reshape(2 * shards, PAD // 2, 2, TILE),
        ("grp", "tp", "role"),
        split_axis=0,
        concat_axis=0,
        tiled=True,
        axis_index_groups=groups,
    )
    rows = shards * PAD
    return pl.pallas_call(
        grad_kernel,
        out_shape=jax.ShapeDtypeStruct((DS, 2 * TILE), BF16),
        in_specs=[VMEM] * 4 + [HBM],
        out_specs=HBM,
        scratch_shapes=[
            pltpu.VMEM((2 * rows, TILE), F32),
            pltpu.VMEM((DS, count), BF16),
            pltpu.VMEM((DS, 2 * TILE), BF16),
            pltpu.SemaphoreType.DMA((2, 8)),
        ],
        compiler_params=params(52),
        cost_estimate=pl.CostEstimate(flops=1000000000, bytes_accessed=7000000, transcendentals=0),
        name="grad",
    )(arrived.reshape(2 * rows, TILE), student_out, pick, spread, stash)


def solution(mesh):
    placed = (
        P("grp", ("tp", "role")),
        P(("tp", "role")),
        P(),
        P(("tp", "role"), None, None, None),
        P("grp", None),
        P("grp", None),
        P(),
        P(None, ("tp", "role")),
    )
    return jax.shard_map(
        on_device, mesh=mesh, in_specs=placed, out_specs=P("grp", ("tp", "role")), check_vma=False
    )
```

time: 91 us -> 86.4 us (0.949)
  blocking collectives: 50.1 us -> 19.7 us
  waiting for transfers between devices: 3.77 us -> 22.1 us
  Pallas kernels: 13.4 us -> 20.6 us
  starting transfers between devices: 17.1 us -> 23.7 us
  local copies, waits for them, and re-layouts: 6.21 us -> 0.01 us
    all_to_all x1 -> x0, blocking collectives: 30.3 us -> none  [on_device(): lax.all_to_all(packed.reshape(shards, PAD, TILE), 'grp', split_axis=0, co...]
    all_to_all x0 -> x1, starting transfers between devices: none -> 21.8 us  [on_device(): lax.all_to_all(packed.reshape(2 * shards, PAD // 2, 2, TILE), ('grp', 'tp...]
    all_to_all x0 -> x1, waiting for transfers between devices: none -> 20.8 us  [on_device(): lax.all_to_all(packed.reshape(2 * shards, PAD // 2, 2, TILE), ('grp', 'tp...]
    ppermute x1 -> x0, starting transfers between devices: 15.1 us -> none  [on_device(): far = lax.ppermute(half, 'tp', [(n, (n + 4) % 8) for n in range(8)])]
    unnamed x16 -> x4, local copies, waits for them, and re-layouts: 6.21 us -> 0.01 us
    pallas_call x4, Pallas kernels: 10.6 us -> 14.7 us  [the longest x1 6.35 us: on_device(): pl.pallas_call(student_kernel, out_shape=(jax.ShapeDtypeStruct((count, 2...]
    pallas_call x1, Pallas kernels: 2.52 us -> 5.68 us  [on_device(): pl.pallas_call(teacher_kernel, out_shape=(jax.ShapeDtypeStruct((16 * TOK...]
    ppermute x1, waiting for transfers between devices: 2.63 us -> 1.21 us  [on_device(): recv = lax.ppermute(send, 'role', [(0, 1), (1, 0)])]
  transfers between devices with their start and end apart: 2 -> 2, of which waited for: 2 -> 2; matrix products, arithmetic and copies ran while one was open for 0% -> 0% of each run, Pallas kernels for 7% -> 9%
where the time goes in v2:
time: 86.4 us; the launch traced here: 86.1 us
  starting transfers between devices  23.7 us (27%)
  waiting for transfers between devices  22.1 us (26%)
  Pallas kernels  20.6 us (24%)
  blocking collectives  19.7 us (23%)
    all_to_all x1, starting transfers between devices, on_device(): lax.all_to_all(packed.reshape(2 * shards, PAD // 2, 2, TILE), ('grp', 'tp...  21.8 us
    all_to_all x1, waiting for transfers between devices, on_device(): lax.all_to_all(packed.reshape(2 * shards, PAD // 2, 2, TILE), ('grp', 'tp...  20.8 us
    all_to_all x1, blocking collectives, on_device(): lax.all_to_all(line, 'tp', 0, 0, tiled=True, axis_index_groups=groups)  19.7 us
    pallas_call x1, Pallas kernels, on_device(): pl.pallas_call(student_kernel, out_shape=(jax.ShapeDtypeStruct((count, 2...  6.35 us
    pallas_call x1, Pallas kernels, on_device(): pl.pallas_call(teacher_kernel, out_shape=(jax.ShapeDtypeStruct((16 * TOK...  5.68 us
    pallas_call x1, Pallas kernels, on_device(): pl.pallas_call(grad_kernel, out_shape=jax.ShapeDtypeStruct((DS, 2 * TILE)...  5.36 us
    ppermute x1, starting transfers between devices, on_device(): recv = lax.ppermute(send, 'role', [(0, 1), (1, 0)])  1.92 us
  transfers between devices with their start and end apart: 2, of which 2 were waited for; matrix products, arithmetic and copies ran while one was open for 0% of the time, Pallas kernels for 9%

profile of v2, /device:TPU:8, one launch (start us, length us, event | category | flops | bytes accessed | tf_op | source)
XLA Modules:
  0.0 86.1 jit_solution(4879034136686931057)
XLA Ops:
  0.0 0.0 copy-start
  0.0 5.7 %teacher.1 = (bf16[4112,128]{1,0:T(8,128)(2,1)}, f32[144,256,128]{2,1,0:T(8,128)}) custom-call(s32[8,128]{1,0:T(8,128)} %bitcast.9, bf16[256,1024]{1,0:T(8,128)(2,1)} %rows_hbm.1, f32[1,1024]{1,0:T(1,128)} %bitcast.10, bf16[8,8,128,128]{3,2,1,0:T(8,128)(2,1)} %tiles_hbm.1), custom_call_target="tpu_custom_call" | custom-call | flops 540000000 | bytes 6000000 | tf_op jit(solution)/shard_map/teacher/pallas_call | solution.py:275
  5.7 1.9 %collective-permute-start = (bf16[4112,128]{1,0:T(8,128)(2,1)}, bf16[4112,128]{1,0:T(8,128)(2,1)S(1)}, u32[]{:S(2)}, u32[]{:S(2)}) collective-permute-start(bf16[4112,128]{1,0:T(8,128)(2,1)} %get-tuple-element.34), channel_id=1, source_target_pairs={{0,1},{1,0},{2,3},{3,2},{4,5},{5,4},{6,7},{7,6},{8,9},{9,8},{10,11... | collective-permute-start | bytes 3158024 | tf_op jit(solution)/shard_map/ppermute | solution.py:297
  7.6 0.0 copy-done
  7.6 1.6 %route.1 = (bf16[1056,512]{1,0:T(8,128)(2,1)S(1)}, s32[8,256]{1,0:T(8,128)S(1)}, bf16[48,256]{1,0:T(8,128)(2,1)S(1)}, f32[16,128]{1,0:T(8,128)S(1)}, f32[16,256,128]{2,1,0:T(8,128)S(1)}) custom-call(s32[1,256]{1,0:T(1,128)S(1)} %bitcast.7, f32[144,256,128]{2,1,0:T(8,128)} %get-tuple-element.28.keep_hbm), custom_call_target="tpu_custom_call" | custom-call | flops 100000000 | bytes 4000000 | tf_op jit(solution)/shard_map/route/pallas_call | solution.py:299
  9.2 1.2 %collective-permute-done.recv_ref = bf16[4112,128]{1,0:T(8,128)(2,1)S(1)} collective-permute-done((bf16[4112,128]{1,0:T(8,128)(2,1)}, bf16[4112,128]{1,0:T(8,128)(2,1)S(1)}, u32[]{:S(2)}, u32[]{:S(2)}) %collective-permute-start) | collective-permute-done | bytes 1052704 | tf_op jit(solution)/shard_map/ppermute | solution.py:297
  10.5 0.2 chip.1
  10.6 19.7 %all_to_all.10.recv_ref = bf16[4,1040,128]{2,1,0:T(8,128)(2,1)S(1)} all-to-all(bf16[4,1040,128]{2,1,0:T(8,128)(2,1)S(1)} %chip.1), channel_id=1, replica_groups={{0,2,4,6},{8,10,12,14},{1,3,5,7},{9,11,13,15},{16,18,20,22},{24,26,28,3..., dimensions={0} | all-to-all | bytes 2129920 | tf_op jit(solution)/shard_map/all_to_all | solution.py:328
  30.3 0.0 copy-start.1
  30.3 1.4 %pack.1 = bf16[2112,128]{1,0:T(8,128)(2,1)} custom-call(bf16[4,1040,128]{2,1,0:T(8,128)(2,1)S(1)} %all_to_all.10.recv_ref, bf16[1056,512]{1,0:T(8,128)(2,1)S(1)} %get-tuple-element.38.place_ref, s32[8,256]{1,0:T(8,128)S(1)} %get-tuple-element.39.rank_ref, bf16[48,256]{1,0:T(8,128)(2,1)S(1)} %get-tuple-element.40.hits_ref), custom_call_target="tpu_custom_call" | custom-call | flops 400000000 | bytes 2000000 | tf_op jit(solution)/shard_map/pack/pallas_call | solution.py:329
  31.7 21.8 %all-to-all-start.1 = ((bf16[96,11,2,128]{3,2,1,0:T(2,128)(2,1)}), bf16[96,11,2,128]{3,2,1,0:T(2,128)(2,1)S(1)}, u32[]{:S(2)}, u32[]{:S(2)}) async-start(bf16[96,11,2,128]{3,2,1,0:T(2,128)(2,1)} %bitcast.3), calls=%async_computation.1 | async-start | bytes 1081344 | tf_op jit(solution)/shard_map/all_to_all | solution.py:364
  53.5 0.0 copy-done.1
  53.5 6.3 %student.1 = (f32[480,256]{1,0:T(8,128)S(1)}, bf16[16384,480]{1,0:T(8,128)(2,1)}, bf16[480,528]{1,0:T(8,128)(2,1)S(1)}, bf16[528,48]{1,0:T(8,128)(2,1)S(1)}) custom-call(bf16[480,4096]{1,0:T(8,128)(2,1)} %rows_ref, f32[1,4096]{1,0:T(1,128)S(1)} %bitcast.8, bf16[4096,256]{1,0:T(8,128)(2,1)} %weight_ref.1), custom_call_target="tpu_custom_call" | custom-call | flops 2000000000 | bytes 10000000 | tf_op jit(solution)/shard_map/student/pallas_call | solution.py:344
  59.9 20.8 %all-to-all-done.1 = bf16[96,11,2,128]{3,2,1,0:T(2,128)(2,1)S(1)} async-done(((bf16[96,11,2,128]{3,2,1,0:T(2,128)(2,1)}), bf16[96,11,2,128]{3,2,1,0:T(2,128)(2,1)S(1)}, u32[]{:S(2)}, u32[]{:S(2)}) %all-to-all-start.1) | async-done | bytes 540704 | tf_op jit(solution)/shard_map/all_to_all | solution.py:364
  80.7 5.4 %grad.1 = bf16[4096,256]{1,0:T(8,128)(2,1)} custom-call(bf16[2112,128]{1,0:T(8,128)(2,1)S(1)} %bitcast.6, f32[480,256]{1,0:T(8,128)S(1)} %get-tuple-element.43.out_ref, bf16[480,528]{1,0:T(8,128)(2,1)S(1)} %get-tuple-element.44.pick_ref, bf16[528,48]{1,0:T(8,128)(2,1)S(1)} %get-tuple-element.45.spread_ref, bf16[16384,480]{1,0:T(8,128)(2,1)} %get-tuple-element.46.stash_hbm), custom_call_target="tpu_custom_call" | custom-call | flops 1000000000 | bytes 7000000 | tf_op jit(solution)/shard_map/grad/pallas_call | solution.py:373
Async XLA Ops:
  0.0 7.6 %copy-start = (s32[256,1]{0,1:T(1,128)S(1)}, s32[256,1]{0,1:T(1,128)}, u32[]{:S(2)}) copy-start(s32[256,1]{0,1:T(1,128)} %param.12) | copy-start | bytes 3076
  5.7 4.8 %collective-permute-start = (bf16[4112,128]{1,0:T(8,128)(2,1)}, bf16[4112,128]{1,0:T(8,128)(2,1)S(1)}, u32[]{:S(2)}, u32[]{:S(2)}) collective-permute-start(bf16[4112,128]{1,0:T(8,128)(2,1)} %get-tuple-element.34), channel_id=1, source_target_pairs={{0,1},{1,0},{2,3},{3,2},{4,5},{5,4},{6,7},{7,6},{8,9},{9,8},{10,11... | collective-permute-start | bytes 3158024 | tf_op jit(solution)/shard_map/ppermute | solution.py:297
  30.3 23.2 %copy-start.1 = (f32[4096]{0:T(1024)S(1)}, f32[4096]{0:T(1024)}, u32[]{:S(2)}) copy-start(f32[4096]{0:T(1024)} %param.14) | copy-start | bytes 49156
  31.7 49.0 %all-to-all-start.1 = ((bf16[96,11,2,128]{3,2,1,0:T(2,128)(2,1)}), bf16[96,11,2,128]{3,2,1,0:T(2,128)(2,1)S(1)}, u32[]{:S(2)}, u32[]{:S(2)}) async-start(bf16[96,11,2,128]{3,2,1,0:T(2,128)(2,1)} %bitcast.3), calls=%async_computation.1 | async-start | bytes 1081344 | tf_op jit(solution)/shard_map/all_to_all | solution.py:364

commit v3 on v2

--- a/solution.py
+++ b/solution.py
@@ -48,7 +48,11 @@
         pltpu.make_async_copy(gain_hbm, gain, sems.at[9]),
         pltpu.make_async_copy(index_hbm, index, sems.at[10]),
     ]
-    loads = [pltpu.make_async_copy(tiles_hbm.at[b], tiles.at[b], sems.at[b]) for b in range(8)]
+    halves = [pl.ds(0, 4), pl.ds(4, 4)]
+    loads = [
+        pltpu.make_async_copy(tiles_hbm.at[part], tiles.at[part], sems.at[n])
+        for n, part in enumerate(halves)
+    ]
     for copy in first + loads:
         copy.start()
     role = lax.axis_index("role")
@@ -62,7 +66,8 @@
         wide = rows[:, lanes].astype(F32)
         squares = squares + wide * wide
         gained = (wide * gain[:, lanes]).astype(BF16)
-        loads[b].wait()
+        if b % 4 == 0:
+            loads[b // 4].wait()
         side = jnp.concatenate([tiles[b, k] for k in range(8)], axis=1)
         products = jnp.dot(gained, side, preferred_element_type=F32)
         for k in range(8):
@@ -175,7 +180,7 @@
 
 
 def student_kernel(
-    rows_ref, gain_ref, weight_ref, out_ref, stash_hbm, pick_ref, spread_ref, turned_ref, sems
+    rows_ref, gain_ref, weight_ref, out_ref, stash_hbm, spread_ref, own_ref, turned_ref, sems
 ):
     step = DS // 8
     count = rows_ref.shape[0]
@@ -197,12 +202,11 @@
             pltpu.make_async_copy(turned_ref.at[here], stash_hbm.at[here], sems.at[n])
         )
         copies[n].start()
-    wanted = lax.broadcasted_iota(jnp.int32, (count, 1), 0)
-    wanted = wanted + wanted // CAP
-    pick_ref[...] = jnp.where(
-        lax.broadcasted_iota(jnp.int32, pick_ref.shape, 1) == wanted, 1.0, 0.0
-    ).astype(BF16)
-    source = lax.broadcasted_iota(jnp.int32, (spread_ref.shape[0], 1), 0) // slots
+    row = lax.broadcasted_iota(jnp.int32, (spread_ref.shape[0], 1), 0)
+    source = row // slots
+    own_ref[...] = jnp.where(
+        lax.broadcasted_iota(jnp.int32, own_ref.shape, 1) == row - source * slots, 1.0, 0.0
+    )
     spread_ref[...] = jnp.where(
         lax.broadcasted_iota(jnp.int32, spread_ref.shape, 1) == source, 1.0, 0.0
     ).astype(BF16)
@@ -211,25 +215,34 @@
 
 
 def grad_kernel(
-    recv_ref, out_ref, pick_ref, spread_ref, stash_hbm, grad_hbm, wide, turned, grad, sems
+    recv_ref, out_ref, spread_ref, own_ref, stash_hbm, grad_hbm, wide, turned, grad, sems
 ):
     steps = sems.shape[1]
     block = DS // steps
     here = [pl.ds(n * block, block) for n in range(steps)]
-    loads = [
-        pltpu.make_async_copy(stash_hbm.at[here[n]], turned.at[here[n]], sems.at[0, n])
-        for n in range(steps)
-    ]
+    loads = {
+        n: pltpu.make_async_copy(
+            stash_hbm.at[pl.ds(n * block, size * block)],
+            turned.at[pl.ds(n * block, size * block)],
+            sems.at[0, n],
+        )
+        for n, size in ((0, 1), (1, 3), (4, 4))
+    }
     stores = [
         pltpu.make_async_copy(grad.at[here[n]], grad_hbm.at[here[n]], sems.at[1, n])
         for n in range(steps)
     ]
-    for copy in loads:
+    for copy in loads.values():
         copy.start()
-    slots = PAD // 2
     half = wide.shape[0] // 2
     count = half // 2
     shards = half // PAD
+    row = lax.broadcasted_iota(jnp.int32, (1, count), 1)
+    source = row // (PAD // 2)
+    row = jnp.where(row - source * (PAD // 2) < CAP, row - source, -1)
+    pick = jnp.where(
+        lax.broadcasted_iota(jnp.int32, (out_ref.shape[0], count), 0) == row, 1.0, 0.0
+    ).astype(BF16)
     wide[...] = recv_ref[...].astype(F32)
 
     def every(start, size, stride):
@@ -242,16 +255,15 @@
     rows = jnp.dot(
         spread_ref[...], jnp.concatenate([high, low], axis=1), preferred_element_type=F32
     )
-    slot = lax.broadcasted_iota(jnp.int32, (count, 1), 0) % slots
-    own = lax.broadcasted_iota(jnp.int32, (count, TILE), 1) == slot
-    scale = jnp.sum(jnp.where(own, rows[:, :TILE] + rows[:, TILE:], 0.0), axis=1, keepdims=True)
+    scale = jnp.sum(own_ref[...] * (rows[:, :TILE] + rows[:, TILE:]), axis=1, keepdims=True)
     targets = jnp.concatenate(
         [(scale * every(j, count, 2)).astype(BF16) for j in range(2)], axis=1
     )
-    wanted = jnp.dot(pick_ref[...], targets, preferred_element_type=F32)
+    wanted = jnp.dot(pick, targets, preferred_element_type=F32)
     delta = ((out_ref[...] - wanted) * (1.0 / math.sqrt(TOK))).astype(BF16)
     for n in range(steps):
-        loads[n].wait()
+        if n in loads:
+            loads[n].wait()
         grad[here[n], :] = jnp.dot(
             turned[here[n], :], delta, preferred_element_type=F32
         ).astype(BF16)
@@ -341,13 +353,13 @@
         name="pack",
     )(line, place, rank, hits)
     student_rows, packed = lax.optimization_barrier((student_rows, packed))
-    student_out, stash, pick, spread = pl.pallas_call(
+    student_out, stash, spread, own = pl.pallas_call(
         student_kernel,
         out_shape=(
             jax.ShapeDtypeStruct((count, 2 * TILE), F32),
             jax.ShapeDtypeStruct((4 * DS, count), BF16),
-            jax.ShapeDtypeStruct((count, shards * PAD // 2), BF16),
             jax.ShapeDtypeStruct((shards * PAD // 2, shards), BF16),
+            jax.ShapeDtypeStruct((shards * PAD // 2, TILE), F32),
         ),
         in_specs=[VMEM] * 3,
         out_specs=(VMEM, HBM, VMEM, VMEM),
@@ -384,7 +396,7 @@
         compiler_params=params(52),
         cost_estimate=pl.CostEstimate(flops=1000000000, bytes_accessed=7000000, transcendentals=0),
         name="grad",
-    )(arrived.reshape(2 * rows, TILE), student_out, pick, spread, stash)
+    )(arrived.reshape(2 * rows, TILE), student_out, spread, own, stash)
 
 
 def solution(mesh):

time: 86.4 us -> 84.6 us (0.979)
  Pallas kernels: 20.6 us -> 18.5 us
    pallas_call x1, Pallas kernels: 5.36 us -> 4.28 us  [on_device(): pl.pallas_call(grad_kernel, out_shape=jax.ShapeDtypeStruct((DS, 2 * TILE)...]
where the time goes in v3:
time: 84.6 us; the launch traced here: 84.3 us
  starting transfers between devices  23.7 us (28%)
  waiting for transfers between devices  22.3 us (26%)
  blocking collectives  19.7 us (23%)
  Pallas kernels  18.5 us (22%)
    all_to_all x1, starting transfers between devices, on_device(): lax.all_to_all(packed.reshape(2 * shards, PAD // 2, 2, TILE), ('grp', 'tp...  21.8 us
    all_to_all x1, waiting for transfers between devices, on_device(): lax.all_to_all(packed.reshape(2 * shards, PAD // 2, 2, TILE), ('grp', 'tp...  21.1 us
    all_to_all x1, blocking collectives, on_device(): lax.all_to_all(line, 'tp', 0, 0, tiled=True, axis_index_groups=groups)  19.7 us
    pallas_call x1, Pallas kernels, on_device(): pl.pallas_call(student_kernel, out_shape=(jax.ShapeDtypeStruct((count, 2...  6.12 us
    pallas_call x1, Pallas kernels, on_device(): pl.pallas_call(teacher_kernel, out_shape=(jax.ShapeDtypeStruct((16 * TOK...  4.95 us
    pallas_call x1, Pallas kernels, on_device(): pl.pallas_call(grad_kernel, out_shape=jax.ShapeDtypeStruct((DS, 2 * TILE)...  4.28 us
    ppermute x1, starting transfers between devices, on_device(): recv = lax.ppermute(send, 'role', [(0, 1), (1, 0)])  1.92 us
  transfers between devices with their start and end apart: 2, of which 2 were waited for; matrix products, arithmetic and copies ran while one was open for 0% of the time, Pallas kernels for 9%

profile of v3, /device:TPU:8, one launch (start us, length us, event | category | flops | bytes accessed | tf_op | source)
XLA Modules:
  0.0 84.3 jit_solution(2612223922820428)
XLA Ops:
  0.0 0.0 copy-start
  0.0 5.0 %teacher.1 = (bf16[4112,128]{1,0:T(8,128)(2,1)}, f32[144,256,128]{2,1,0:T(8,128)}) custom-call(s32[8,128]{1,0:T(8,128)} %bitcast.9, bf16[256,1024]{1,0:T(8,128)(2,1)} %rows_hbm.1, f32[1,1024]{1,0:T(1,128)} %bitcast.10, bf16[8,8,128,128]{3,2,1,0:T(8,128)(2,1)} %tiles_hbm.1), custom_call_target="tpu_custom_call" | custom-call | flops 540000000 | bytes 6000000 | tf_op jit(solution)/shard_map/teacher/pallas_call | solution.py:287
  5.0 1.9 %collective-permute-start = (bf16[4112,128]{1,0:T(8,128)(2,1)}, bf16[4112,128]{1,0:T(8,128)(2,1)S(1)}, u32[]{:S(2)}, u32[]{:S(2)}) collective-permute-start(bf16[4112,128]{1,0:T(8,128)(2,1)} %get-tuple-element.34), channel_id=1, source_target_pairs={{0,1},{1,0},{2,3},{3,2},{4,5},{5,4},{6,7},{7,6},{8,9},{9,8},{10,11... | collective-permute-start | bytes 3158024 | tf_op jit(solution)/shard_map/ppermute | solution.py:309
  6.9 0.0 copy-done
  6.9 1.6 %route.1 = (bf16[1056,512]{1,0:T(8,128)(2,1)S(1)}, s32[8,256]{1,0:T(8,128)S(1)}, bf16[48,256]{1,0:T(8,128)(2,1)S(1)}, f32[16,128]{1,0:T(8,128)S(1)}, f32[16,256,128]{2,1,0:T(8,128)S(1)}) custom-call(s32[1,256]{1,0:T(1,128)S(1)} %bitcast.7, f32[144,256,128]{2,1,0:T(8,128)} %get-tuple-element.28.keep_hbm), custom_call_target="tpu_custom_call" | custom-call | flops 100000000 | bytes 4000000 | tf_op jit(solution)/shard_map/route/pallas_call | solution.py:311
  8.5 1.2 %collective-permute-done.recv_ref = bf16[4112,128]{1,0:T(8,128)(2,1)S(1)} collective-permute-done((bf16[4112,128]{1,0:T(8,128)(2,1)}, bf16[4112,128]{1,0:T(8,128)(2,1)S(1)}, u32[]{:S(2)}, u32[]{:S(2)}) %collective-permute-start) | collective-permute-done | bytes 1052704 | tf_op jit(solution)/shard_map/ppermute | solution.py:309
  9.7 0.2 chip.1
  9.9 19.7 %all_to_all.10.recv_ref = bf16[4,1040,128]{2,1,0:T(8,128)(2,1)S(1)} all-to-all(bf16[4,1040,128]{2,1,0:T(8,128)(2,1)S(1)} %chip.1), channel_id=1, replica_groups={{0,2,4,6},{8,10,12,14},{1,3,5,7},{9,11,13,15},{16,18,20,22},{24,26,28,3..., dimensions={0} | all-to-all | bytes 2129920 | tf_op jit(solution)/shard_map/all_to_all | solution.py:340
  29.6 0.0 copy-start.1
  29.6 1.4 %pack.1 = bf16[2112,128]{1,0:T(8,128)(2,1)} custom-call(bf16[4,1040,128]{2,1,0:T(8,128)(2,1)S(1)} %all_to_all.10.recv_ref, bf16[1056,512]{1,0:T(8,128)(2,1)S(1)} %get-tuple-element.38.place_ref, s32[8,256]{1,0:T(8,128)S(1)} %get-tuple-element.39.rank_ref, bf16[48,256]{1,0:T(8,128)(2,1)S(1)} %get-tuple-element.40.hits_ref), custom_call_target="tpu_custom_call" | custom-call | flops 400000000 | bytes 2000000 | tf_op jit(solution)/shard_map/pack/pallas_call | solution.py:341
  31.0 21.8 %all-to-all-start.1 = ((bf16[96,11,2,128]{3,2,1,0:T(2,128)(2,1)}), bf16[96,11,2,128]{3,2,1,0:T(2,128)(2,1)S(1)}, u32[]{:S(2)}, u32[]{:S(2)}) async-start(bf16[96,11,2,128]{3,2,1,0:T(2,128)(2,1)} %bitcast.3), calls=%async_computation.1 | async-start | bytes 1081344 | tf_op jit(solution)/shard_map/all_to_all | solution.py:376
  52.8 0.0 copy-done.1
  52.8 6.1 %student.1 = (f32[480,256]{1,0:T(8,128)S(1)}, bf16[16384,480]{1,0:T(8,128)(2,1)}, bf16[528,48]{1,0:T(8,128)(2,1)S(1)}, f32[528,128]{1,0:T(8,128)S(1)}) custom-call(bf16[480,4096]{1,0:T(8,128)(2,1)} %rows_ref, f32[1,4096]{1,0:T(1,128)S(1)} %bitcast.8, bf16[4096,256]{1,0:T(8,128)(2,1)} %weight_ref.1), custom_call_target="tpu_custom_call" | custom-call | flops 2000000000 | bytes 10000000 | tf_op jit(solution)/shard_map/student/pallas_call | solution.py:356
  58.9 21.1 %all-to-all-done.1 = bf16[96,11,2,128]{3,2,1,0:T(2,128)(2,1)S(1)} async-done(((bf16[96,11,2,128]{3,2,1,0:T(2,128)(2,1)}), bf16[96,11,2,128]{3,2,1,0:T(2,128)(2,1)S(1)}, u32[]{:S(2)}, u32[]{:S(2)}) %all-to-all-start.1) | async-done | bytes 540704 | tf_op jit(solution)/shard_map/all_to_all | solution.py:376
  80.0 4.3 %grad.1 = bf16[4096,256]{1,0:T(8,128)(2,1)} custom-call(bf16[2112,128]{1,0:T(8,128)(2,1)S(1)} %bitcast.6, f32[480,256]{1,0:T(8,128)S(1)} %get-tuple-element.43.out_ref, bf16[528,48]{1,0:T(8,128)(2,1)S(1)} %get-tuple-element.44.spread_ref, f32[528,128]{1,0:T(8,128)S(1)} %get-tuple-element.45.own_ref, bf16[16384,480]{1,0:T(8,128)(2,1)} %get-tuple-element.46.stash_hbm), custom_call_target="tpu_custom_call" | custom-call | flops 1000000000 | bytes 7000000 | tf_op jit(solution)/shard_map/grad/pallas_call | solution.py:385
Async XLA Ops:
  0.0 6.9 %copy-start = (s32[256,1]{0,1:T(1,128)S(1)}, s32[256,1]{0,1:T(1,128)}, u32[]{:S(2)}) copy-start(s32[256,1]{0,1:T(1,128)} %param.12) | copy-start | bytes 3076
  5.0 4.8 %collective-permute-start = (bf16[4112,128]{1,0:T(8,128)(2,1)}, bf16[4112,128]{1,0:T(8,128)(2,1)S(1)}, u32[]{:S(2)}, u32[]{:S(2)}) collective-permute-start(bf16[4112,128]{1,0:T(8,128)(2,1)} %get-tuple-element.34), channel_id=1, source_target_pairs={{0,1},{1,0},{2,3},{3,2},{4,5},{5,4},{6,7},{7,6},{8,9},{9,8},{10,11... | collective-permute-start | bytes 3158024 | tf_op jit(solution)/shard_map/ppermute | solution.py:309
  29.6 23.2 %copy-start.1 = (f32[4096]{0:T(1024)S(1)}, f32[4096]{0:T(1024)}, u32[]{:S(2)}) copy-start(f32[4096]{0:T(1024)} %param.14) | copy-start | bytes 49156
  31.0 49.0 %all-to-all-start.1 = ((bf16[96,11,2,128]{3,2,1,0:T(2,128)(2,1)}), bf16[96,11,2,128]{3,2,1,0:T(2,128)(2,1)S(1)}, u32[]{:S(2)}, u32[]{:S(2)}) async-start(bf16[96,11,2,128]{3,2,1,0:T(2,128)(2,1)} %bitcast.3), calls=%async_computation.1 | async-start | bytes 1081344 | tf_op jit(solution)/shard_map/all_to_all | solution.py:376

commit v4 on v3

--- a/solution.py
+++ b/solution.py
@@ -179,29 +179,57 @@
         copy.wait()
 
 
-def student_kernel(
-    rows_ref, gain_ref, weight_ref, out_ref, stash_hbm, spread_ref, own_ref, turned_ref, sems
-):
-    step = DS // 8
-    count = rows_ref.shape[0]
-    slots = PAD // 2
+def student_work(rows_hbm, gain_hbm, weight_hbm, out_ref, stash_hbm, rows, gain, weight, turned, sems):
+    steps = 8
+    step = DS // steps
+    loads = [
+        pltpu.make_async_copy(rows_hbm, rows, sems.at[steps]),
+        pltpu.make_async_copy(gain_hbm, gain, sems.at[steps + 1]),
+        pltpu.make_async_copy(weight_hbm, weight, sems.at[steps + 2]),
+    ]
+    for copy in loads:
+        copy.start()
+    count = rows.shape[0]
     squares = jnp.zeros((count, TILE), F32)
+    loads[0].wait()
     for n in range(DS // TILE):
-        wide = rows_ref[:, n * TILE : (n + 1) * TILE].astype(F32)
+        wide = rows[:, n * TILE : (n + 1) * TILE].astype(F32)
         squares = squares + wide * wide
     scale = lax.rsqrt(jnp.sum(squares, axis=1, keepdims=True) / DS + EPS)
     out_ref[...] = jnp.zeros_like(out_ref)
+    loads[1].wait()
+    loads[2].wait()
     copies = []
-    for n in range(DS // step):
+    for n in range(steps):
         part = slice(n * step, (n + 1) * step)
-        normed = (rows_ref[:, part].astype(F32) * scale * gain_ref[:, part]).astype(BF16)
-        out_ref[...] += jnp.dot(normed, weight_ref[part, :], preferred_element_type=F32)
-        turned_ref[part, :] = jnp.transpose(normed)
+        normed = (rows[:, part].astype(F32) * scale * gain[:, part]).astype(BF16)
+        out_ref[...] += jnp.dot(normed, weight[part, :], preferred_element_type=F32)
+        turned[part, :] = jnp.transpose(normed)
         here = pl.ds(n * step, step)
-        copies.append(
-            pltpu.make_async_copy(turned_ref.at[here], stash_hbm.at[here], sems.at[n])
-        )
+        copies.append(pltpu.make_async_copy(turned.at[here], stash_hbm.at[here], sems.at[n]))
         copies[n].start()
+    for copy in copies:
+        copy.wait()
+
+
+def early_student_kernel(rows_hbm, gain_hbm, weight_hbm, line_ref, out_ref, stash_hbm, *scratch):
+    @pl.when(lax.axis_index("role") == 0)
+    def _():
+        student_work(rows_hbm, gain_hbm, weight_hbm, out_ref, stash_hbm, *scratch)
+
+
+def late_student_kernel(
+    rows_hbm, gain_hbm, weight_hbm, early_ref, early_hbm, out_ref, stash_hbm, spread_ref, own_ref, *scratch
+):
+    @pl.when(lax.axis_index("role") == 0)
+    def _():
+        out_ref[...] = early_ref[...]
+
+    @pl.when(lax.axis_index("role") == 1)
+    def _():
+        student_work(rows_hbm, gain_hbm, weight_hbm, out_ref, stash_hbm, *scratch)
+
+    slots = PAD // 2
     row = lax.broadcasted_iota(jnp.int32, (spread_ref.shape[0], 1), 0)
     source = row // slots
     own_ref[...] = jnp.where(
@@ -210,8 +238,6 @@
     spread_ref[...] = jnp.where(
         lax.broadcasted_iota(jnp.int32, spread_ref.shape, 1) == source, 1.0, 0.0
     ).astype(BF16)
-    for copy in copies:
-        copy.wait()
 
 
 def grad_kernel(
@@ -336,6 +362,29 @@
         cost_estimate=pl.CostEstimate(flops=1000000, bytes_accessed=4000000, transcendentals=0),
         name="chip",
     )(tail, keep, recv)
+    student_inputs = (student_rows, student_gain[None, :], student_weight)
+    student_shapes = (
+        jax.ShapeDtypeStruct((count, 2 * TILE), F32),
+        jax.ShapeDtypeStruct((4 * DS, count), BF16),
+    )
+    student_scratch = [
+        pltpu.VMEM(student_rows.shape, BF16),
+        pltpu.VMEM((1, DS), F32),
+        pltpu.VMEM(student_weight.shape, BF16),
+        pltpu.VMEM((DS, count), BF16),
+        pltpu.SemaphoreType.DMA((11,)),
+    ]
+    early, stash = pl.pallas_call(
+        early_student_kernel,
+        out_shape=student_shapes,
+        in_specs=[HBM] * 3 + [VMEM],
+        out_specs=(VMEM, HBM),
+        scratch_shapes=student_scratch,
+        compiler_params=params(52),
+        cost_estimate=pl.CostEstimate(flops=2000000000, bytes_accessed=10000000, transcendentals=480),
+        name="early_student",
+    )(*student_inputs, line)
+    early, stash, line = lax.optimization_barrier((early, stash, line))
     groups = [[z * 4 + x for x in range(4)] for z in range(2)]
     line = lax.all_to_all(line, "tp", 0, 0, tiled=True, axis_index_groups=groups)
     packed = pl.pallas_call(
@@ -352,22 +401,22 @@
         cost_estimate=pl.CostEstimate(flops=400000000, bytes_accessed=2000000, transcendentals=0),
         name="pack",
     )(line, place, rank, hits)
-    student_rows, packed = lax.optimization_barrier((student_rows, packed))
+    early, stash, packed = lax.optimization_barrier((early, stash, packed))
     student_out, stash, spread, own = pl.pallas_call(
-        student_kernel,
+        late_student_kernel,
         out_shape=(
-            jax.ShapeDtypeStruct((count, 2 * TILE), F32),
-            jax.ShapeDtypeStruct((4 * DS, count), BF16),
+            *student_shapes,
             jax.ShapeDtypeStruct((shards * PAD // 2, shards), BF16),
             jax.ShapeDtypeStruct((shards * PAD // 2, TILE), F32),
         ),
-        in_specs=[VMEM] * 3,
+        in_specs=[HBM] * 3 + [VMEM, HBM],
         out_specs=(VMEM, HBM, VMEM, VMEM),
-        scratch_shapes=[pltpu.VMEM((DS, count), BF16), pltpu.SemaphoreType.DMA((8,))],
+        input_output_aliases={4: 1},
+        scratch_shapes=student_scratch,
         compiler_params=params(52),
         cost_estimate=pl.CostEstimate(flops=2000000000, bytes_accessed=10000000, transcendentals=480),
-        name="student",
-    )(student_rows, student_gain[None, :], student_weight)
+        name="late_student",
+    )(*student_inputs, early, stash)
     groups = [
         [(g * 8 + z * 4 + x) * 2 + c for z in range(2) for g in range(shards)]
         for x in range(4)

time: 84.6 us -> 80.5 us (0.952)
  blocking collectives: 19.7 us -> 15.1 us
    all_to_all x1, blocking collectives: 19.7 us -> 15.1 us  [on_device(): lax.all_to_all(line, 'tp', 0, 0, tiled=True, axis_index_groups=groups)]
    pallas_call x1 -> x2, Pallas kernels: 6.12 us -> 5.68 us  [the longest x1 5.42 us: on_device(): pl.pallas_call(early_student_kernel, out_shape=student_shapes, in_specs=[...]
  transfers between devices with their start and end apart: 2 -> 2, of which waited for: 2 -> 2; matrix products, arithmetic and copies ran while one was open for 0% -> 0% of each run, Pallas kernels for 9% -> 2%
where the time goes in v4:
time: 80.5 us; the launch traced here: 80.1 us
  starting transfers between devices  23.7 us (29%)
  waiting for transfers between devices  22.6 us (28%)
  Pallas kernels  18.2 us (23%)
  blocking collectives  15.1 us (19%)
    all_to_all x1, starting transfers between devices, on_device(): lax.all_to_all(packed.reshape(2 * shards, PAD // 2, 2, TILE), ('grp', 'tp...  21.8 us
    all_to_all x1, waiting for transfers between devices, on_device(): lax.all_to_all(packed.reshape(2 * shards, PAD // 2, 2, TILE), ('grp', 'tp...  21.4 us
    all_to_all x1, blocking collectives, on_device(): lax.all_to_all(line, 'tp', 0, 0, tiled=True, axis_index_groups=groups)  15.1 us
    pallas_call x1, Pallas kernels, on_device(): pl.pallas_call(early_student_kernel, out_shape=student_shapes, in_specs=[...  5.42 us
    pallas_call x1, Pallas kernels, on_device(): pl.pallas_call(teacher_kernel, out_shape=(jax.ShapeDtypeStruct((16 * TOK...  4.95 us
    pallas_call x1, Pallas kernels, on_device(): pl.pallas_call(grad_kernel, out_shape=jax.ShapeDtypeStruct((DS, 2 * TILE)...  4.28 us
    ppermute x1, starting transfers between devices, on_device(): recv = lax.ppermute(send, 'role', [(0, 1), (1, 0)])  1.92 us
    pallas_call x1, Pallas kernels, on_device(): pl.pallas_call(route_kernel, out_shape=(jax.ShapeDtypeStruct((shards * PA...  1.61 us
  transfers between devices with their start and end apart: 2, of which 2 were waited for; matrix products, arithmetic and copies ran while one was open for 0% of the time, Pallas kernels for 2%

profile of v4, /device:TPU:8, one launch (start us, length us, event | category | flops | bytes accessed | tf_op | source)
XLA Modules:
  0.0 80.1 jit_solution(7066751222337537328)
XLA Ops:
  0.0 0.0 copy-start.1
  0.0 5.0 %teacher.1 = (bf16[4112,128]{1,0:T(8,128)(2,1)}, f32[144,256,128]{2,1,0:T(8,128)}) custom-call(s32[8,128]{1,0:T(8,128)} %bitcast.10, bf16[256,1024]{1,0:T(8,128)(2,1)} %rows_hbm.3, f32[1,1024]{1,0:T(1,128)} %bitcast.11, bf16[8,8,128,128]{3,2,1,0:T(8,128)(2,1)} %tiles_hbm.1), custom_call_target="tpu_custom_call" | custom-call | flops 540000000 | bytes 6000000 | tf_op jit(solution)/shard_map/teacher/pallas_call | solution.py:313
  5.0 1.9 %collective-permute-start = (bf16[4112,128]{1,0:T(8,128)(2,1)}, bf16[4112,128]{1,0:T(8,128)(2,1)S(1)}, u32[]{:S(2)}, u32[]{:S(2)}) collective-permute-start(bf16[4112,128]{1,0:T(8,128)(2,1)} %get-tuple-element.40), channel_id=1, source_target_pairs={{0,1},{1,0},{2,3},{3,2},{4,5},{5,4},{6,7},{7,6},{8,9},{9,8},{10,11... | collective-permute-start | bytes 3158024 | tf_op jit(solution)/shard_map/ppermute | solution.py:335
  6.9 0.0 copy-done.1
  6.9 1.6 %route.1 = (bf16[1056,512]{1,0:T(8,128)(2,1)S(1)}, s32[8,256]{1,0:T(8,128)S(1)}, bf16[48,256]{1,0:T(8,128)(2,1)S(1)}, f32[16,128]{1,0:T(8,128)S(1)}, f32[16,256,128]{2,1,0:T(8,128)S(1)}) custom-call(s32[1,256]{1,0:T(1,128)S(1)} %bitcast.9, f32[144,256,128]{2,1,0:T(8,128)} %get-tuple-element.34.keep_hbm), custom_call_target="tpu_custom_call" | custom-call | flops 100000000 | bytes 4000000 | tf_op jit(solution)/shard_map/route/pallas_call | solution.py:337
  8.5 1.2 %collective-permute-done.recv_ref = bf16[4112,128]{1,0:T(8,128)(2,1)S(1)} collective-permute-done((bf16[4112,128]{1,0:T(8,128)(2,1)}, bf16[4112,128]{1,0:T(8,128)(2,1)S(1)}, u32[]{:S(2)}, u32[]{:S(2)}) %collective-permute-start) | collective-permute-done | bytes 1052704 | tf_op jit(solution)/shard_map/ppermute | solution.py:335
  9.7 0.0 copy-start
  9.7 0.2 chip.1.line_ref
  10.0 0.5 copy-done
  10.5 5.4 %early_student.1 = (f32[480,256]{1,0:T(8,128)S(1)}, bf16[16384,480]{1,0:T(8,128)(2,1)}) custom-call(bf16[480,4096]{1,0:T(8,128)(2,1)} %rows_hbm.5, f32[1,4096]{1,0:T(1,128)S(1)} %bitcast.7, bf16[4096,256]{1,0:T(8,128)(2,1)} %weight_hbm.3, bf16[4,1040,128]{2,1,0:T(8,128)(2,1)S(1)} %chip.1.line_ref), custom_call_target="tpu_custom_call" | custom-call | flops 2000000000 | bytes 10000000 | tf_op jit(solution)/shard_map/early_student/pallas_call | solution.py:377
  15.9 15.1 %all_to_all.10.recv_ref = bf16[4,1040,128]{2,1,0:T(8,128)(2,1)S(1)} all-to-all(bf16[4,1040,128]{2,1,0:T(8,128)(2,1)S(1)} %chip.1.line_ref), channel_id=1, replica_groups={{0,2,4,6},{8,10,12,14},{1,3,5,7},{9,11,13,15},{16,18,20,22},{24,26,28,3..., dimensions={0} | all-to-all | bytes 2129920 | tf_op jit(solution)/shard_map/all_to_all | solution.py:389
  31.0 1.4 %pack.1 = bf16[2112,128]{1,0:T(8,128)(2,1)} custom-call(bf16[4,1040,128]{2,1,0:T(8,128)(2,1)S(1)} %all_to_all.10.recv_ref, bf16[1056,512]{1,0:T(8,128)(2,1)S(1)} %get-tuple-element.49.place_ref, s32[8,256]{1,0:T(8,128)S(1)} %get-tuple-element.50.rank_ref, bf16[48,256]{1,0:T(8,128)(2,1)S(1)} %get-tuple-element.51.hits_ref), custom_call_target="tpu_custom_call" | custom-call | flops 400000000 | bytes 2000000 | tf_op jit(solution)/shard_map/pack/pallas_call | solution.py:390
  32.4 21.8 %all-to-all-start.1 = ((bf16[96,11,2,128]{3,2,1,0:T(2,128)(2,1)}), bf16[96,11,2,128]{3,2,1,0:T(2,128)(2,1)S(1)}, u32[]{:S(2)}, u32[]{:S(2)}) async-start(bf16[96,11,2,128]{3,2,1,0:T(2,128)(2,1)} %bitcast.4), calls=%async_computation.1 | async-start | bytes 1081344 | tf_op jit(solution)/shard_map/all_to_all | solution.py:425
  54.2 0.3 late_student.1
  54.4 21.4 %all-to-all-done.1 = bf16[96,11,2,128]{3,2,1,0:T(2,128)(2,1)S(1)} async-done(((bf16[96,11,2,128]{3,2,1,0:T(2,128)(2,1)}), bf16[96,11,2,128]{3,2,1,0:T(2,128)(2,1)S(1)}, u32[]{:S(2)}, u32[]{:S(2)}) %all-to-all-start.1) | async-done | bytes 540704 | tf_op jit(solution)/shard_map/all_to_all | solution.py:425
  75.8 4.3 %grad.1 = bf16[4096,256]{1,0:T(8,128)(2,1)} custom-call(bf16[2112,128]{1,0:T(8,128)(2,1)S(1)} %bitcast.6, f32[480,256]{1,0:T(8,128)S(1)} %get-tuple-element.55.out_ref, bf16[528,48]{1,0:T(8,128)(2,1)S(1)} %get-tuple-element.56.spread_ref, f32[528,128]{1,0:T(8,128)S(1)} %get-tuple-element.57.own_ref, bf16[16384,480]{1,0:T(8,128)(2,1)} %get-tuple-element.58.stash_hbm), custom_call_target="tpu_custom_call" | custom-call | flops 1000000000 | bytes 7000000 | tf_op jit(solution)/shard_map/grad/pallas_call | solution.py:434
Async XLA Ops:
  0.0 6.9 %copy-start.1 = (s32[256,1]{0,1:T(1,128)S(1)}, s32[256,1]{0,1:T(1,128)}, u32[]{:S(2)}) copy-start(s32[256,1]{0,1:T(1,128)} %param.12) | copy-start | bytes 3076
  5.0 4.8 %collective-permute-start = (bf16[4112,128]{1,0:T(8,128)(2,1)}, bf16[4112,128]{1,0:T(8,128)(2,1)S(1)}, u32[]{:S(2)}, u32[]{:S(2)}) collective-permute-start(bf16[4112,128]{1,0:T(8,128)(2,1)} %get-tuple-element.40), channel_id=1, source_target_pairs={{0,1},{1,0},{2,3},{3,2},{4,5},{5,4},{6,7},{7,6},{8,9},{9,8},{10,11... | collective-permute-start | bytes 3158024 | tf_op jit(solution)/shard_map/ppermute | solution.py:335
  9.7 0.7 copy-start
  32.4 43.5 %all-to-all-start.1 = ((bf16[96,11,2,128]{3,2,1,0:T(2,128)(2,1)}), bf16[96,11,2,128]{3,2,1,0:T(2,128)(2,1)S(1)}, u32[]{:S(2)}, u32[]{:S(2)}) async-start(bf16[96,11,2,128]{3,2,1,0:T(2,128)(2,1)} %bitcast.4), calls=%async_computation.1 | async-start | bytes 1081344 | tf_op jit(solution)/shard_map/all_to_all | solution.py:425

commit v5 on v4

--- a/solution.py
+++ b/solution.py
@@ -116,7 +116,7 @@
 
 
 def route_kernel(
-    shard_ref, keep_hbm, place_ref, rank_ref, hits_ref, tail_ref, keep_ref, sems
+    shard_ref, gain_ref, keep_hbm, place_ref, rank_ref, hits_ref, tail_ref, keep_ref, held_ref, sems
 ):
     copies = [
         pltpu.make_async_copy(keep_hbm.at[pl.ds(0, 16)], keep_ref, sems.at[0]),
@@ -124,6 +124,7 @@
     ]
     for copy in copies:
         copy.start()
+    held_ref[...] = gain_ref[...]
     dest = shard_ref[...]
     hits = jnp.where(lax.broadcasted_iota(jnp.int32, hits_ref.shape, 0) == dest, 1.0, 0.0)
     hits_ref[...] = hits.astype(BF16)
@@ -144,7 +145,7 @@
         copy.wait()
 
 
-def pack_kernel(recv_ref, place_ref, rank_ref, hits_ref, out_hbm, wide, out, sems):
+def pack_kernel(recv_ref, place_ref, rank_ref, hits_ref, out_ref, wide):
     tail = slice(4 * TOK, 4 * TOK + TAIL)
 
     def total(n):
@@ -169,23 +170,15 @@
         )
         for z in range(2):
             wide[pl.ds(z * rows + 2 * CAP + n, shown.shape[0], stride=PAD), :] = shown
-    copies = []
-    for z in range(2):
-        here = pl.ds(z * rows, rows)
-        out[here, :] = wide[here, :].astype(BF16)
-        copies.append(pltpu.make_async_copy(out.at[here], out_hbm.at[here], sems.at[z]))
-        copies[z].start()
-    for copy in copies:
-        copy.wait()
-
-
-def student_work(rows_hbm, gain_hbm, weight_hbm, out_ref, stash_hbm, rows, gain, weight, turned, sems):
+    out_ref[...] = wide[...].astype(BF16)
+
+
+def student_work(rows_hbm, gain, weight_hbm, out_ref, stash_hbm, rows, weight, turned, sems):
     steps = 8
     step = DS // steps
     loads = [
         pltpu.make_async_copy(rows_hbm, rows, sems.at[steps]),
-        pltpu.make_async_copy(gain_hbm, gain, sems.at[steps + 1]),
-        pltpu.make_async_copy(weight_hbm, weight, sems.at[steps + 2]),
+        pltpu.make_async_copy(weight_hbm, weight, sems.at[steps + 1]),
     ]
     for copy in loads:
         copy.start()
@@ -198,7 +191,6 @@
     scale = lax.rsqrt(jnp.sum(squares, axis=1, keepdims=True) / DS + EPS)
     out_ref[...] = jnp.zeros_like(out_ref)
     loads[1].wait()
-    loads[2].wait()
     copies = []
     for n in range(steps):
         part = slice(n * step, (n + 1) * step)
@@ -212,36 +204,22 @@
         copy.wait()
 
 
-def early_student_kernel(rows_hbm, gain_hbm, weight_hbm, line_ref, out_ref, stash_hbm, *scratch):
+def early_student_kernel(rows_hbm, gain_ref, weight_hbm, line_ref, out_ref, stash_hbm, *scratch):
     @pl.when(lax.axis_index("role") == 0)
     def _():
-        student_work(rows_hbm, gain_hbm, weight_hbm, out_ref, stash_hbm, *scratch)
+        student_work(rows_hbm, gain_ref, weight_hbm, out_ref, stash_hbm, *scratch)
 
 
 def late_student_kernel(
-    rows_hbm, gain_hbm, weight_hbm, early_ref, early_hbm, out_ref, stash_hbm, spread_ref, own_ref, *scratch
+    rows_hbm, gain_ref, weight_hbm, recv_ref, early_hbm, out_ref, stash_hbm, *scratch
 ):
-    @pl.when(lax.axis_index("role") == 0)
-    def _():
-        out_ref[...] = early_ref[...]
-
     @pl.when(lax.axis_index("role") == 1)
     def _():
-        student_work(rows_hbm, gain_hbm, weight_hbm, out_ref, stash_hbm, *scratch)
-
-    slots = PAD // 2
-    row = lax.broadcasted_iota(jnp.int32, (spread_ref.shape[0], 1), 0)
-    source = row // slots
-    own_ref[...] = jnp.where(
-        lax.broadcasted_iota(jnp.int32, own_ref.shape, 1) == row - source * slots, 1.0, 0.0
-    )
-    spread_ref[...] = jnp.where(
-        lax.broadcasted_iota(jnp.int32, spread_ref.shape, 1) == source, 1.0, 0.0
-    ).astype(BF16)
+        student_work(rows_hbm, gain_ref, weight_hbm, out_ref, stash_hbm, *scratch)
 
 
 def grad_kernel(
-    recv_ref, out_ref, spread_ref, own_ref, stash_hbm, grad_hbm, wide, turned, grad, sems
+    recv_ref, early_ref, late_ref, stash_hbm, grad_hbm, wide, turned, grad, sems
 ):
     steps = sems.shape[1]
     block = DS // steps
@@ -263,11 +241,17 @@
     half = wide.shape[0] // 2
     count = half // 2
     shards = half // PAD
+    row = lax.broadcasted_iota(jnp.int32, (count, 1), 0)
+    source = row // (PAD // 2)
+    own = lax.broadcasted_iota(jnp.int32, (count, TILE), 1) == row - source * (PAD // 2)
+    spread = jnp.where(
+        lax.broadcasted_iota(jnp.int32, (count, shards), 1) == source, 1.0, 0.0
+    ).astype(BF16)
     row = lax.broadcasted_iota(jnp.int32, (1, count), 1)
     source = row // (PAD // 2)
     row = jnp.where(row - source * (PAD // 2) < CAP, row - source, -1)
     pick = jnp.where(
-        lax.broadcasted_iota(jnp.int32, (out_ref.shape[0], count), 0) == row, 1.0, 0.0
+        lax.broadcasted_iota(jnp.int32, (early_ref.shape[0], count), 0) == row, 1.0, 0.0
     ).astype(BF16)
     wide[...] = recv_ref[...].astype(F32)
 
@@ -279,14 +263,17 @@
     high = inv.astype(BF16)
     low = (inv - high.astype(F32)).astype(BF16)
     rows = jnp.dot(
-        spread_ref[...], jnp.concatenate([high, low], axis=1), preferred_element_type=F32
-    )
-    scale = jnp.sum(own_ref[...] * (rows[:, :TILE] + rows[:, TILE:]), axis=1, keepdims=True)
+        spread, jnp.concatenate([high, low], axis=1), preferred_element_type=F32
+    )
+    scale = jnp.sum(
+        jnp.where(own, rows[:, :TILE] + rows[:, TILE:], 0.0), axis=1, keepdims=True
+    )
     targets = jnp.concatenate(
         [(scale * every(j, count, 2)).astype(BF16) for j in range(2)], axis=1
     )
     wanted = jnp.dot(pick, targets, preferred_element_type=F32)
-    delta = ((out_ref[...] - wanted) * (1.0 / math.sqrt(TOK))).astype(BF16)
+    student_out = jnp.where(lax.axis_index("role") == 0, early_ref[...], late_ref[...])
+    delta = ((student_out - wanted) * (1.0 / math.sqrt(TOK))).astype(BF16)
     for n in range(steps):
         if n in loads:
             loads[n].wait()
@@ -333,8 +320,10 @@
         name="teacher",
     )(block_index.T, teacher_rows, teacher_gain[None, :], block_tiles)
     recv = lax.ppermute(send, "role", [(0, 1), (1, 0)])
-    student_shard, keep = lax.optimization_barrier((student_shard, keep))
-    place, rank, hits, tail, keep = pl.pallas_call(
+    student_shard, student_gain, keep = lax.optimization_barrier(
+        (student_shard, student_gain, keep)
+    )
+    place, rank, hits, tail, keep, gain = pl.pallas_call(
         route_kernel,
         out_shape=(
             jax.ShapeDtypeStruct((shards * PAD, 2 * TOK), BF16),
@@ -342,16 +331,17 @@
             jax.ShapeDtypeStruct((shards, TOK), BF16),
             jax.ShapeDtypeStruct((TAIL, TILE), F32),
             jax.ShapeDtypeStruct((16, TOK, TILE), F32),
+            jax.ShapeDtypeStruct((1, DS), F32),
         ),
-        in_specs=[VMEM, HBM],
-        out_specs=(VMEM,) * 5,
+        in_specs=[VMEM, VMEM, HBM],
+        out_specs=(VMEM,) * 6,
         scratch_shapes=[pltpu.SemaphoreType.DMA((2,))],
         compiler_params=params(ROUTE_MIB),
         cost_estimate=pl.CostEstimate(flops=100000000, bytes_accessed=4000000, transcendentals=0),
         name="route",
-    )(student_shard.reshape(1, TOK), keep)
-    place, rank, hits, tail, keep, recv = lax.optimization_barrier(
-        (place, rank, hits, tail, keep, recv)
+    )(student_shard.reshape(1, TOK), student_gain[None, :], keep)
+    place, rank, hits, tail, keep, gain, recv = lax.optimization_barrier(
+        (place, rank, hits, tail, keep, gain, recv)
     )
     line = pl.pallas_call(
         chip_kernel,
@@ -362,22 +352,21 @@
         cost_estimate=pl.CostEstimate(flops=1000000, bytes_accessed=4000000, transcendentals=0),
         name="chip",
     )(tail, keep, recv)
-    student_inputs = (student_rows, student_gain[None, :], student_weight)
+    student_inputs = (student_rows, gain, student_weight)
     student_shapes = (
         jax.ShapeDtypeStruct((count, 2 * TILE), F32),
         jax.ShapeDtypeStruct((4 * DS, count), BF16),
     )
     student_scratch = [
         pltpu.VMEM(student_rows.shape, BF16),
-        pltpu.VMEM((1, DS), F32),
         pltpu.VMEM(student_weight.shape, BF16),
         pltpu.VMEM((DS, count), BF16),
-        pltpu.SemaphoreType.DMA((11,)),
+        pltpu.SemaphoreType.DMA((10,)),
     ]
     early, stash = pl.pallas_call(
         early_student_kernel,
         out_shape=student_shapes,
-        in_specs=[HBM] * 3 + [VMEM],
+        in_specs=[HBM, VMEM, HBM, VMEM],
         out_specs=(VMEM, HBM),
         scratch_shapes=student_scratch,
         compiler_params=params(52),
@@ -391,32 +380,12 @@
         pack_kernel,
         out_shape=jax.ShapeDtypeStruct((2 * shards * PAD, TILE), BF16),
         in_specs=[VMEM] * 4,
-        out_specs=HBM,
-        scratch_shapes=[
-            pltpu.VMEM((2 * shards * PAD, TILE), F32),
-            pltpu.VMEM((2 * shards * PAD, TILE), BF16),
-            pltpu.SemaphoreType.DMA((2,)),
-        ],
+        out_specs=VMEM,
+        scratch_shapes=[pltpu.VMEM((2 * shards * PAD, TILE), F32)],
         compiler_params=params(),
         cost_estimate=pl.CostEstimate(flops=400000000, bytes_accessed=2000000, transcendentals=0),
         name="pack",
     )(line, place, rank, hits)
-    early, stash, packed = lax.optimization_barrier((early, stash, packed))
-    student_out, stash, spread, own = pl.pallas_call(
-        late_student_kernel,
-        out_shape=(
-            *student_shapes,
-            jax.ShapeDtypeStruct((shards * PAD // 2, shards), BF16),
-            jax.ShapeDtypeStruct((shards * PAD // 2, TILE), F32),
-        ),
-        in_specs=[HBM] * 3 + [VMEM, HBM],
-        out_specs=(VMEM, HBM, VMEM, VMEM),
-        input_output_aliases={4: 1},
-        scratch_shapes=student_scratch,
-        compiler_params=params(52),
-        cost_estimate=pl.CostEstimate(flops=2000000000, bytes_accessed=10000000, transcendentals=480),
-        name="late_student",
-    )(*student_inputs, early, stash)
     groups = [
         [(g * 8 + z * 4 + x) * 2 + c for z in range(2) for g in range(shards)]
         for x in range(4)
@@ -431,10 +400,22 @@
         axis_index_groups=groups,
     )
     rows = shards * PAD
+    arrived = arrived.reshape(2 * rows, TILE)
+    late, stash = pl.pallas_call(
+        late_student_kernel,
+        out_shape=student_shapes,
+        in_specs=[HBM, VMEM, HBM, VMEM, HBM],
+        out_specs=(VMEM, HBM),
+        input_output_aliases={4: 1},
+        scratch_shapes=student_scratch,
+        compiler_params=params(52),
+        cost_estimate=pl.CostEstimate(flops=2000000000, bytes_accessed=10000000, transcendentals=480),
+        name="late_student",
+    )(*student_inputs, arrived, stash)
     return pl.pallas_call(
         grad_kernel,
         out_shape=jax.ShapeDtypeStruct((DS, 2 * TILE), BF16),
-        in_specs=[VMEM] * 4 + [HBM],
+        in_specs=[VMEM] * 3 + [HBM],
         out_specs=HBM,
         scratch_shapes=[
             pltpu.VMEM((2 * rows, TILE), F32),
@@ -445,7 +426,7 @@
         compiler_params=params(52),
         cost_estimate=pl.CostEstimate(flops=1000000000, bytes_accessed=7000000, transcendentals=0),
         name="grad",
-    )(arrived.reshape(2 * rows, TILE), student_out, spread, own, stash)
+    )(arrived, early, late, stash)
 
 
 def solution(mesh):

time: 80.5 us -> 78.9 us (0.980)
  blocking collectives: 15.1 us -> 58.3 us
  starting transfers between devices: 23.7 us -> 1.92 us
  waiting for transfers between devices: 22.6 us -> 1.2 us
  Pallas kernels: 18.2 us -> 17.1 us
    all_to_all x0 -> x1, blocking collectives: none -> 43.3 us  [on_device(): lax.all_to_all(packed.reshape(2 * shards, PAD // 2, 2, TILE), ('grp', 'tp...]
    all_to_all x1 -> x0, starting transfers between devices: 21.8 us -> none  [on_device(): lax.all_to_all(packed.reshape(2 * shards, PAD // 2, 2, TILE), ('grp', 'tp...]
    all_to_all x1 -> x0, waiting for transfers between devices: 21.4 us -> none  [on_device(): lax.all_to_all(packed.reshape(2 * shards, PAD // 2, 2, TILE), ('grp', 'tp...]
    pallas_call x1, Pallas kernels: 1.41 us -> 0.6 us  [on_device(): pl.pallas_call(pack_kernel, out_shape=jax.ShapeDtypeStruct((2 * shards *...]
  transfers between devices with their start and end apart: 2 -> 1, of which waited for: 2 -> 1; matrix products, arithmetic and copies ran while one was open for 0% -> 0% of each run, Pallas kernels for 2% -> 2%
where the time goes in v5:
time: 78.9 us; the launch traced here: 78.6 us
  blocking collectives  58.3 us (74%)
  Pallas kernels  17.1 us (22%)
  starting transfers between devices  1.92 us (2%)
  waiting for transfers between devices  1.2 us (2%)
    all_to_all x1, blocking collectives, on_device(): lax.all_to_all(packed.reshape(2 * shards, PAD // 2, 2, TILE), ('grp', 'tp...  43.3 us
    all_to_all x1, blocking collectives, on_device(): lax.all_to_all(line, 'tp', 0, 0, tiled=True, axis_index_groups=groups)  15.1 us
    pallas_call x1, Pallas kernels, on_device(): pl.pallas_call(early_student_kernel, out_shape=student_shapes, in_specs=[...  5.38 us
    pallas_call x1, Pallas kernels, on_device(): pl.pallas_call(teacher_kernel, out_shape=(jax.ShapeDtypeStruct((16 * TOK...  4.97 us
    pallas_call x1, Pallas kernels, on_device(): pl.pallas_call(grad_kernel, out_shape=jax.ShapeDtypeStruct((DS, 2 * TILE)...  4.18 us
    ppermute x1, starting transfers between devices, on_device(): recv = lax.ppermute(send, 'role', [(0, 1), (1, 0)])  1.92 us
    pallas_call x1, Pallas kernels, on_device(): pl.pallas_call(route_kernel, out_shape=(jax.ShapeDtypeStruct((shards * PA...  1.61 us
  transfers between devices with their start and end apart: 1, of which 1 were waited for; matrix products, arithmetic and copies ran while one was open for 0% of the time, Pallas kernels for 2%

profile of v5, /device:TPU:8, one launch (start us, length us, event | category | flops | bytes accessed | tf_op | source)
XLA Modules:
  0.0 78.6 jit_solution(14907959544402436688)
XLA Ops:
  0.0 0.0 copy-start
  0.0 0.0 copy-start.1
  0.0 5.0 %teacher.1 = (bf16[4112,128]{1,0:T(8,128)(2,1)}, f32[144,256,128]{2,1,0:T(8,128)}) custom-call(s32[8,128]{1,0:T(8,128)} %bitcast.11, bf16[256,1024]{1,0:T(8,128)(2,1)} %rows_hbm.3, f32[1,1024]{1,0:T(1,128)} %bitcast.12, bf16[8,8,128,128]{3,2,1,0:T(8,128)(2,1)} %tiles_hbm.1), custom_call_target="tpu_custom_call" | custom-call | flops 540000000 | bytes 6000000 | tf_op jit(solution)/shard_map/teacher/pallas_call | solution.py:300
  5.0 1.9 %collective-permute-start = (bf16[4112,128]{1,0:T(8,128)(2,1)}, bf16[4112,128]{1,0:T(8,128)(2,1)S(1)}, u32[]{:S(2)}, u32[]{:S(2)}) collective-permute-start(bf16[4112,128]{1,0:T(8,128)(2,1)} %get-tuple-element.40), channel_id=1, source_target_pairs={{0,1},{1,0},{2,3},{3,2},{4,5},{5,4},{6,7},{7,6},{8,9},{9,8},{10,11... | collective-permute-start | bytes 3158024 | tf_op jit(solution)/shard_map/ppermute | solution.py:322
  6.9 0.0 copy-done
  6.9 0.0 copy-done.1
  6.9 1.6 %route.1 = (bf16[1056,512]{1,0:T(8,128)(2,1)S(1)}, s32[8,256]{1,0:T(8,128)S(1)}, bf16[48,256]{1,0:T(8,128)(2,1)S(1)}, f32[16,128]{1,0:T(8,128)S(1)}, f32[16,256,128]{2,1,0:T(8,128)S(1)}, /*index=5*/f32[1,4096]{1,0:T(1,128)S(1)}) custom-call(s32[1,256]{1,0:T(1,128)S(1)} %bitcast.10, f32[1,4096]{1,0:T(1,128)S(1)} %bitcast.9, ...), custom_call_target="tpu_custom_call" | custom-call | flops 100000000 | bytes 4000000 | tf_op jit(solution)/shard_map/route/pallas_call | solution.py:326
  8.5 1.2 %collective-permute-done.recv_ref = bf16[4112,128]{1,0:T(8,128)(2,1)S(1)} collective-permute-done((bf16[4112,128]{1,0:T(8,128)(2,1)}, bf16[4112,128]{1,0:T(8,128)(2,1)S(1)}, u32[]{:S(2)}, u32[]{:S(2)}) %collective-permute-start) | collective-permute-done | bytes 1052704 | tf_op jit(solution)/shard_map/ppermute | solution.py:322
  9.8 0.2 chip.1.line_ref
  10.0 5.4 %early_student.1 = (f32[480,256]{1,0:T(8,128)S(1)}, bf16[16384,480]{1,0:T(8,128)(2,1)}) custom-call(bf16[480,4096]{1,0:T(8,128)(2,1)} %rows_hbm.5, f32[1,4096]{1,0:T(1,128)S(1)} %get-tuple-element.41.gain_ref, bf16[4096,256]{1,0:T(8,128)(2,1)} %weight_hbm.3, bf16[4,1040,128]{2,1,0:T(8,128)(2,1)S(1)} %chip.1.line_ref), custom_call_target="tpu_custom_call" | custom-call | flops 2000000000 | bytes 10000000 | tf_op jit(solution)/shard_map/early_student/pallas_call | solution.py:366
  15.4 15.1 %all_to_all.10.recv_ref = bf16[4,1040,128]{2,1,0:T(8,128)(2,1)S(1)} all-to-all(bf16[4,1040,128]{2,1,0:T(8,128)(2,1)S(1)} %chip.1.line_ref), channel_id=1, replica_groups={{0,2,4,6},{8,10,12,14},{1,3,5,7},{9,11,13,15},{16,18,20,22},{24,26,28,3..., dimensions={0} | all-to-all | bytes 2129920 | tf_op jit(solution)/shard_map/all_to_all | solution.py:378
  30.4 0.6 pack.1
  31.1 43.3 %all_to_all.11 = bf16[96,11,2,128]{3,2,1,0:T(2,128)(2,1)S(1)} all-to-all(bf16[96,11,2,128]{3,2,1,0:T(2,128)(2,1)S(1)} %bitcast.8), channel_id=1, replica_groups={{0,16,32,48,64,80,96,112,128,144,160,176,192,208,224,240,256,272,288,30..., dimensions={0} | all-to-all | bytes 1081344 | tf_op jit(solution)/shard_map/all_to_all | solution.py:394
  74.3 0.1 late_student.1
  74.4 4.2 %grad.1 = bf16[4096,256]{1,0:T(8,128)(2,1)} custom-call(bf16[2112,128]{1,0:T(8,128)(2,1)S(1)} %bitcast.7, f32[480,256]{1,0:T(8,128)S(1)} %get-tuple-element.51.early_ref, f32[480,256]{1,0:T(8,128)S(1)} %get-tuple-element.53.late_ref, bf16[16384,480]{1,0:T(8,128)(2,1)} %get-tuple-element.54.stash_hbm), custom_call_target="tpu_custom_call" | custom-call | flops 1000000000 | bytes 7000000 | tf_op jit(solution)/shard_map/grad/pallas_call | solution.py:415
Async XLA Ops:
  0.0 6.9 %copy-start = (f32[4096]{0:T(1024)S(1)}, f32[4096]{0:T(1024)}, u32[]{:S(2)}) copy-start(f32[4096]{0:T(1024)} %param.14) | copy-start | bytes 49156
  0.0 6.9 %copy-start.1 = (s32[256,1]{0,1:T(1,128)S(1)}, s32[256,1]{0,1:T(1,128)}, u32[]{:S(2)}) copy-start(s32[256,1]{0,1:T(1,128)} %param.12) | copy-start | bytes 3076
  5.0 4.8 %collective-permute-start = (bf16[4112,128]{1,0:T(8,128)(2,1)}, bf16[4112,128]{1,0:T(8,128)(2,1)S(1)}, u32[]{:S(2)}, u32[]{:S(2)}) collective-permute-start(bf16[4112,128]{1,0:T(8,128)(2,1)} %get-tuple-element.40), channel_id=1, source_target_pairs={{0,1},{1,0},{2,3},{3,2},{4,5},{5,4},{6,7},{7,6},{8,9},{9,8},{10,11... | collective-permute-start | bytes 3158024 | tf_op jit(solution)/shard_map/ppermute | solution.py:322

commit v6 on v5

--- a/solution.py
+++ b/solution.py
@@ -170,7 +170,7 @@
         )
         for z in range(2):
             wide[pl.ds(z * rows + 2 * CAP + n, shown.shape[0], stride=PAD), :] = shown
-    out_ref[...] = wide[...].astype(BF16)
+    out_ref[...] = wide[: 2 * rows, :].astype(BF16)
 
 
 def student_work(rows_hbm, gain, weight_hbm, out_ref, stash_hbm, rows, weight, turned, sems):
@@ -204,10 +204,15 @@
         copy.wait()
 
 
-def early_student_kernel(rows_hbm, gain_ref, weight_hbm, line_ref, out_ref, stash_hbm, *scratch):
+def early_student_kernel(
+    rows_hbm, gain_ref, weight_hbm, line_ref, out_ref, stash_hbm, head_ref, rows, weight, turned, sems
+):
     @pl.when(lax.axis_index("role") == 0)
     def _():
-        student_work(rows_hbm, gain_ref, weight_hbm, out_ref, stash_hbm, *scratch)
+        student_work(
+            rows_hbm, gain_ref, weight_hbm, out_ref, stash_hbm, rows, weight, turned, sems
+        )
+        head_ref[...] = turned[: head_ref.shape[0], :]
 
 
 def late_student_kernel(
@@ -219,7 +224,7 @@
 
 
 def grad_kernel(
-    recv_ref, early_ref, late_ref, stash_hbm, grad_hbm, wide, turned, grad, sems
+    recv_ref, early_ref, late_ref, head_ref, stash_hbm, grad_hbm, wide, turned, grad, sems
 ):
     steps = sems.shape[1]
     block = DS // steps
@@ -236,9 +241,20 @@
         pltpu.make_async_copy(grad.at[here[n]], grad_hbm.at[here[n]], sems.at[1, n])
         for n in range(steps)
     ]
-    for copy in loads.values():
-        copy.start()
-    half = wide.shape[0] // 2
+    early_core = lax.axis_index("role") == 0
+    for n, copy in loads.items():
+        if n:
+            copy.start()
+
+    @pl.when(jnp.logical_not(early_core))
+    def _():
+        loads[0].start()
+
+    @pl.when(early_core)
+    def _():
+        turned[:block, :] = head_ref[...]
+
+    half = recv_ref.shape[0] // 2
     count = half // 2
     shards = half // PAD
     row = lax.broadcasted_iota(jnp.int32, (count, 1), 0)
@@ -253,7 +269,7 @@
     pick = jnp.where(
         lax.broadcasted_iota(jnp.int32, (early_ref.shape[0], count), 0) == row, 1.0, 0.0
     ).astype(BF16)
-    wide[...] = recv_ref[...].astype(F32)
+    wide[: 2 * half, :] = recv_ref[...].astype(F32)
 
     def every(start, size, stride):
         return sum(wide[pl.ds(z * half + start, size, stride=stride), :] for z in range(2))
@@ -272,10 +288,15 @@
         [(scale * every(j, count, 2)).astype(BF16) for j in range(2)], axis=1
     )
     wanted = jnp.dot(pick, targets, preferred_element_type=F32)
-    student_out = jnp.where(lax.axis_index("role") == 0, early_ref[...], late_ref[...])
+    student_out = jnp.where(early_core, early_ref[...], late_ref[...])
     delta = ((student_out - wanted) * (1.0 / math.sqrt(TOK))).astype(BF16)
+
+    @pl.when(jnp.logical_not(early_core))
+    def _():
+        loads[0].wait()
+
     for n in range(steps):
-        if n in loads:
+        if n and n in loads:
             loads[n].wait()
         grad[here[n], :] = jnp.dot(
             turned[here[n], :], delta, preferred_element_type=F32
@@ -363,17 +384,17 @@
         pltpu.VMEM((DS, count), BF16),
         pltpu.SemaphoreType.DMA((10,)),
     ]
-    early, stash = pl.pallas_call(
+    early, stash, head = pl.pallas_call(
         early_student_kernel,
-        out_shape=student_shapes,
+        out_shape=(*student_shapes, jax.ShapeDtypeStruct((DS // 8, count), BF16)),
         in_specs=[HBM, VMEM, HBM, VMEM],
-        out_specs=(VMEM, HBM),
+        out_specs=(VMEM, HBM, VMEM),
         scratch_shapes=student_scratch,
-        compiler_params=params(52),
+        compiler_params=params(51),
         cost_estimate=pl.CostEstimate(flops=2000000000, bytes_accessed=10000000, transcendentals=480),
         name="early_student",
     )(*student_inputs, line)
-    early, stash, line = lax.optimization_barrier((early, stash, line))
+    early, stash, head, line = lax.optimization_barrier((early, stash, head, line))
     groups = [[z * 4 + x for x in range(4)] for z in range(2)]
     line = lax.all_to_all(line, "tp", 0, 0, tiled=True, axis_index_groups=groups)
     packed = pl.pallas_call(
@@ -381,7 +402,7 @@
         out_shape=jax.ShapeDtypeStruct((2 * shards * PAD, TILE), BF16),
         in_specs=[VMEM] * 4,
         out_specs=VMEM,
-        scratch_shapes=[pltpu.VMEM((2 * shards * PAD, TILE), F32)],
+        scratch_shapes=[pltpu.VMEM((2 * shards * PAD + 2 * TAIL, TILE), F32)],
         compiler_params=params(),
         cost_estimate=pl.CostEstimate(flops=400000000, bytes_accessed=2000000, transcendentals=0),
         name="pack",
@@ -408,25 +429,25 @@
         out_specs=(VMEM, HBM),
         input_output_aliases={4: 1},
         scratch_shapes=student_scratch,
-        compiler_params=params(52),
+        compiler_params=params(51),
         cost_estimate=pl.CostEstimate(flops=2000000000, bytes_accessed=10000000, transcendentals=480),
         name="late_student",
     )(*student_inputs, arrived, stash)
     return pl.pallas_call(
         grad_kernel,
         out_shape=jax.ShapeDtypeStruct((DS, 2 * TILE), BF16),
-        in_specs=[VMEM] * 3 + [HBM],
+        in_specs=[VMEM] * 4 + [HBM],
         out_specs=HBM,
         scratch_shapes=[
-            pltpu.VMEM((2 * rows, TILE), F32),
+            pltpu.VMEM((2 * rows + 2 * TAIL, TILE), F32),
             pltpu.VMEM((DS, count), BF16),
             pltpu.VMEM((DS, 2 * TILE), BF16),
             pltpu.SemaphoreType.DMA((2, 8)),
         ],
-        compiler_params=params(52),
+        compiler_params=params(51),
         cost_estimate=pl.CostEstimate(flops=1000000000, bytes_accessed=7000000, transcendentals=0),
         name="grad",
-    )(arrived, early, late, stash)
+    )(arrived, early, late, head, stash)
 
 
 def solution(mesh):

time: 78.9 us -> 78.4 us (level)
  no operation moved by 1% of the time
where the time goes in v6:
time: 78.4 us; the launch traced here: 78.2 us
  blocking collectives  58.3 us (74%)
  Pallas kernels  16.7 us (21%)
  starting transfers between devices  1.92 us (2%)
  waiting for transfers between devices  1.2 us (2%)
    all_to_all x1, blocking collectives, on_device(): lax.all_to_all(packed.reshape(2 * shards, PAD // 2, 2, TILE), ('grp', 'tp...  43.3 us
    all_to_all x1, blocking collectives, on_device(): lax.all_to_all(line, 'tp', 0, 0, tiled=True, axis_index_groups=groups)  15.1 us
    pallas_call x1, Pallas kernels, on_device(): pl.pallas_call(early_student_kernel, out_shape=(*student_shapes, jax.Shap...  5.41 us
    pallas_call x1, Pallas kernels, on_device(): pl.pallas_call(teacher_kernel, out_shape=(jax.ShapeDtypeStruct((16 * TOK...  4.97 us
    pallas_call x1, Pallas kernels, on_device(): pl.pallas_call(grad_kernel, out_shape=jax.ShapeDtypeStruct((DS, 2 * TILE)...  3.73 us
    ppermute x1, starting transfers between devices, on_device(): recv = lax.ppermute(send, 'role', [(0, 1), (1, 0)])  1.92 us
    pallas_call x1, Pallas kernels, on_device(): pl.pallas_call(route_kernel, out_shape=(jax.ShapeDtypeStruct((shards * PA...  1.61 us
  transfers between devices with their start and end apart: 1, of which 1 were waited for; matrix products, arithmetic and copies ran while one was open for 0% of the time, Pallas kernels for 2%

profile of v6, /device:TPU:8, one launch (start us, length us, event | category | flops | bytes accessed | tf_op | source)
XLA Modules:
  0.0 78.2 jit_solution(8252822399786926114)
XLA Ops:
  0.0 0.0 copy-start
  0.0 0.0 copy-start.1
  0.0 5.0 %teacher.1 = (bf16[4112,128]{1,0:T(8,128)(2,1)}, f32[144,256,128]{2,1,0:T(8,128)}) custom-call(s32[8,128]{1,0:T(8,128)} %bitcast.11, bf16[256,1024]{1,0:T(8,128)(2,1)} %rows_hbm.3, f32[1,1024]{1,0:T(1,128)} %bitcast.12, bf16[8,8,128,128]{3,2,1,0:T(8,128)(2,1)} %tiles_hbm.1), custom_call_target="tpu_custom_call" | custom-call | flops 540000000 | bytes 6000000 | tf_op jit(solution)/shard_map/teacher/pallas_call | solution.py:321
  5.0 1.9 %collective-permute-start = (bf16[4112,128]{1,0:T(8,128)(2,1)}, bf16[4112,128]{1,0:T(8,128)(2,1)S(1)}, u32[]{:S(2)}, u32[]{:S(2)}) collective-permute-start(bf16[4112,128]{1,0:T(8,128)(2,1)} %get-tuple-element.42), channel_id=1, source_target_pairs={{0,1},{1,0},{2,3},{3,2},{4,5},{5,4},{6,7},{7,6},{8,9},{9,8},{10,11... | collective-permute-start | bytes 3158024 | tf_op jit(solution)/shard_map/ppermute | solution.py:343
  6.9 0.0 copy-done
  6.9 0.0 copy-done.1
  6.9 1.6 %route.1 = (bf16[1056,512]{1,0:T(8,128)(2,1)S(1)}, s32[8,256]{1,0:T(8,128)S(1)}, bf16[48,256]{1,0:T(8,128)(2,1)S(1)}, f32[16,128]{1,0:T(8,128)S(1)}, f32[16,256,128]{2,1,0:T(8,128)S(1)}, /*index=5*/f32[1,4096]{1,0:T(1,128)S(1)}) custom-call(s32[1,256]{1,0:T(1,128)S(1)} %bitcast.10, f32[1,4096]{1,0:T(1,128)S(1)} %bitcast.9, ...), custom_call_target="tpu_custom_call" | custom-call | flops 100000000 | bytes 4000000 | tf_op jit(solution)/shard_map/route/pallas_call | solution.py:347
  8.5 1.2 %collective-permute-done.recv_ref = bf16[4112,128]{1,0:T(8,128)(2,1)S(1)} collective-permute-done((bf16[4112,128]{1,0:T(8,128)(2,1)}, bf16[4112,128]{1,0:T(8,128)(2,1)S(1)}, u32[]{:S(2)}, u32[]{:S(2)}) %collective-permute-start) | collective-permute-done | bytes 1052704 | tf_op jit(solution)/shard_map/ppermute | solution.py:343
  9.8 0.2 chip.1.line_ref
  10.0 5.4 %early_student.1 = (f32[480,256]{1,0:T(8,128)S(1)}, bf16[16384,480]{1,0:T(8,128)(2,1)}, bf16[512,480]{1,0:T(8,128)(2,1)S(1)}) custom-call(bf16[480,4096]{1,0:T(8,128)(2,1)} %rows_hbm.5, f32[1,4096]{1,0:T(1,128)S(1)} %get-tuple-element.43.gain_ref, bf16[4096,256]{1,0:T(8,128)(2,1)} %weight_hbm.3, bf16[4,1040,128]{2,1,0:T(8,128)(2,1)S(1)} %chip.1.line_ref), custom_call_target="tpu_custom_call" | custom-call | flops 2000000000 | bytes 10000000 | tf_op jit(solution)/shard_map/early_student/pallas_call | solution.py:387
  15.4 15.1 %all_to_all.10.recv_ref = bf16[4,1040,128]{2,1,0:T(8,128)(2,1)S(1)} all-to-all(bf16[4,1040,128]{2,1,0:T(8,128)(2,1)S(1)} %chip.1.line_ref), channel_id=1, replica_groups={{0,2,4,6},{8,10,12,14},{1,3,5,7},{9,11,13,15},{16,18,20,22},{24,26,28,3..., dimensions={0} | all-to-all | bytes 2129920 | tf_op jit(solution)/shard_map/all_to_all | solution.py:399
  30.5 0.6 pack.1
  31.1 43.3 %all_to_all.11 = bf16[96,11,2,128]{3,2,1,0:T(2,128)(2,1)S(1)} all-to-all(bf16[96,11,2,128]{3,2,1,0:T(2,128)(2,1)S(1)} %bitcast.8), channel_id=1, replica_groups={{0,16,32,48,64,80,96,112,128,144,160,176,192,208,224,240,256,272,288,30..., dimensions={0} | all-to-all | bytes 1081344 | tf_op jit(solution)/shard_map/all_to_all | solution.py:415
  74.3 0.1 late_student.1
  74.4 3.7 %grad.1 = bf16[4096,256]{1,0:T(8,128)(2,1)} custom-call(bf16[2112,128]{1,0:T(8,128)(2,1)S(1)} %bitcast.7, f32[480,256]{1,0:T(8,128)S(1)} %get-tuple-element.54.early_ref, f32[480,256]{1,0:T(8,128)S(1)} %get-tuple-element.56.late_ref, bf16[512,480]{1,0:T(8,128)(2,1)S(1)} %get-tuple-element.57.head_ref, bf16[16384,480]{1,0:T(8,128)(2,1)} %get-tuple-element.58.stash_hbm), custom_call_target="tpu_custom_call" | custom-call | flops 1000000000 | bytes 7000000 | tf_op jit(solution)/shard_map/grad/pallas_call | solution.py:436
Async XLA Ops:
  0.0 6.9 %copy-start = (f32[4096]{0:T(1024)S(1)}, f32[4096]{0:T(1024)}, u32[]{:S(2)}) copy-start(f32[4096]{0:T(1024)} %param.14) | copy-start | bytes 49156
  0.0 6.9 %copy-start.1 = (s32[256,1]{0,1:T(1,128)S(1)}, s32[256,1]{0,1:T(1,128)}, u32[]{:S(2)}) copy-start(s32[256,1]{0,1:T(1,128)} %param.12) | copy-start | bytes 3076
  5.0 4.8 %collective-permute-start = (bf16[4112,128]{1,0:T(8,128)(2,1)}, bf16[4112,128]{1,0:T(8,128)(2,1)S(1)}, u32[]{:S(2)}, u32[]{:S(2)}) collective-permute-start(bf16[4112,128]{1,0:T(8,128)(2,1)} %get-tuple-element.42), channel_id=1, source_target_pairs={{0,1},{1,0},{2,3},{3,2},{4,5},{5,4},{6,7},{7,6},{8,9},{9,8},{10,11... | collective-permute-start | bytes 3158024 | tf_op jit(solution)/shard_map/ppermute | solution.py:343

commit v7 on v6

--- a/solution.py
+++ b/solution.py
@@ -20,7 +20,7 @@
 PAD = 22
 TEACHER_MIB = 58
 ROUTE_MIB = 46
-STASH = 144
+STASH = 288
 TAIL = 16
 
 
@@ -41,7 +41,7 @@
 
 def teacher_kernel(
     index_hbm, rows_hbm, gain_hbm, tiles_hbm, send_hbm, keep_hbm,
-    index, rows, gain, tiles, acc, send, own_sums, sems
+    index, rows, gain, tiles, acc, send, held, own_sums, sems
 ):
     first = [
         pltpu.make_async_copy(rows_hbm, rows, sems.at[8]),
@@ -75,9 +75,9 @@
             own = 1 - jnp.bitwise_xor((c >> 1) & 1, role)
             place = own * 16 + ((c >> 2) & 3) * 4 + (c >> 4) * 2 + (c & 1)
             acc[place] += products[:, k * TILE : (k + 1) * TILE]
-    stores = [
-        pltpu.make_async_copy(acc.at[pl.ds(16, 16)], keep_hbm.at[pl.ds(0, 16)], sems.at[11])
-    ]
+    for n in range(16):
+        held[n] = acc[16 + n].astype(BF16)
+    stores = [pltpu.make_async_copy(held, keep_hbm.at[pl.ds(0, 16)], sems.at[11])]
     stores[0].start()
     sums = jnp.sum(squares, axis=1, keepdims=True) * (1.0 / DT)
     row = jnp.concatenate(
@@ -87,7 +87,7 @@
         ],
         axis=0,
     )
-    own_sums[...] = jnp.concatenate([row, jnp.zeros((TAIL - 2, TILE), F32)], axis=0)
+    own_sums[...] = pack_sums(row)
     stores.append(
         pltpu.make_async_copy(own_sums, keep_hbm.at[16, pl.ds(0, TAIL)], sems.at[16])
     )
@@ -105,12 +105,12 @@
 
 
 def chip_kernel(tail_ref, keep_ref, recv_ref, out_ref):
-    tail = pack_sums(tail_ref[0:2] + read_sums(recv_ref[16 * TOK :, :]))
+    tail = pack_sums(read_sums(tail_ref[...]) + read_sums(recv_ref[16 * TOK :, :]))
     for x in range(4):
         for n in range(4):
             m = x * 4 + n
             out_ref[x, n * TOK : (n + 1) * TOK, :] = (
-                keep_ref[m] + recv_ref[m * TOK : (m + 1) * TOK, :].astype(F32)
+                keep_ref[m].astype(F32) + recv_ref[m * TOK : (m + 1) * TOK, :].astype(F32)
             ).astype(BF16)
         out_ref[x, 4 * TOK :, :] = tail
 
@@ -176,21 +176,28 @@
 def student_work(rows_hbm, gain, weight_hbm, out_ref, stash_hbm, rows, weight, turned, sems):
     steps = 8
     step = DS // steps
+    count = rows.shape[0]
+    halves = [pl.ds(0, count // 2), pl.ds(count // 2, count // 2)]
     loads = [
-        pltpu.make_async_copy(rows_hbm, rows, sems.at[steps]),
-        pltpu.make_async_copy(weight_hbm, weight, sems.at[steps + 1]),
-    ]
-    for copy in loads:
-        copy.start()
-    count = rows.shape[0]
-    squares = jnp.zeros((count, TILE), F32)
-    loads[0].wait()
-    for n in range(DS // TILE):
-        wide = rows[:, n * TILE : (n + 1) * TILE].astype(F32)
-        squares = squares + wide * wide
-    scale = lax.rsqrt(jnp.sum(squares, axis=1, keepdims=True) / DS + EPS)
+        pltpu.make_async_copy(rows_hbm.at[part], rows.at[part], sems.at[steps + n])
+        for n, part in enumerate(halves)
+    ]
+    loads.append(pltpu.make_async_copy(weight_hbm, weight, sems.at[steps + 2]))
+    loads[0].start()
+    loads[1].start()
+    scale = []
+    for part, copy in zip(halves, loads):
+        copy.wait()
+        if not scale:
+            loads[2].start()
+        squares = jnp.zeros((count // 2, TILE), F32)
+        for n in range(DS // TILE):
+            wide = rows[part, n * TILE : (n + 1) * TILE].astype(F32)
+            squares = squares + wide * wide
+        scale.append(lax.rsqrt(jnp.sum(squares, axis=1, keepdims=True) / DS + EPS))
+    scale = jnp.concatenate(scale, axis=0)
     out_ref[...] = jnp.zeros_like(out_ref)
-    loads[1].wait()
+    loads[2].wait()
     copies = []
     for n in range(steps):
         part = slice(n * step, (n + 1) * step)
@@ -322,7 +329,7 @@
         teacher_kernel,
         out_shape=(
             jax.ShapeDtypeStruct((16 * TOK + TAIL, TILE), BF16),
-            jax.ShapeDtypeStruct((STASH, TOK, TILE), F32),
+            jax.ShapeDtypeStruct((STASH, TOK, TILE), BF16),
         ),
         in_specs=[HBM] * 4,
         out_specs=(HBM, HBM),
@@ -333,7 +340,8 @@
             pltpu.VMEM(block_tiles.shape, BF16),
             pltpu.VMEM((32, TOK, TILE), F32),
             pltpu.VMEM((16 * TOK + TAIL, TILE), BF16),
-            pltpu.VMEM((TAIL, TILE), F32),
+            pltpu.VMEM((16, TOK, TILE), BF16),
+            pltpu.VMEM((TAIL, TILE), BF16),
             pltpu.SemaphoreType.DMA((17,)),
         ],
         compiler_params=params(TEACHER_MIB),
@@ -350,8 +358,8 @@
             jax.ShapeDtypeStruct((shards * PAD, 2 * TOK), BF16),
             jax.ShapeDtypeStruct((8, TOK), jnp.int32),
             jax.ShapeDtypeStruct((shards, TOK), BF16),
-            jax.ShapeDtypeStruct((TAIL, TILE), F32),
-            jax.ShapeDtypeStruct((16, TOK, TILE), F32),
+            jax.ShapeDtypeStruct((TAIL, TILE), BF16),
+            jax.ShapeDtypeStruct((16, TOK, TILE), BF16),
             jax.ShapeDtypeStruct((1, DS), F32),
         ),
         in_specs=[VMEM, VMEM, HBM],
@@ -382,7 +390,7 @@
         pltpu.VMEM(student_rows.shape, BF16),
         pltpu.VMEM(student_weight.shape, BF16),
         pltpu.VMEM((DS, count), BF16),
-        pltpu.SemaphoreType.DMA((10,)),
+        pltpu.SemaphoreType.DMA((11,)),
     ]
     early, stash, head = pl.pallas_call(
         early_student_kernel,

time: 78.4 us -> 78.2 us (level)
  no operation moved by 1% of the time
where the time goes in v7:
time: 78.2 us; the launch traced here: 78 us
  blocking collectives  57.9 us (74%)
  Pallas kernels  16.5 us (21%)
  starting transfers between devices  1.92 us (2%)
  waiting for transfers between devices  1.57 us (2%)
    all_to_all x1, blocking collectives, on_device(): lax.all_to_all(packed.reshape(2 * shards, PAD // 2, 2, TILE), ('grp', 'tp...  42.8 us
    all_to_all x1, blocking collectives, on_device(): lax.all_to_all(line, 'tp', 0, 0, tiled=True, axis_index_groups=groups)  15.1 us
    pallas_call x1, Pallas kernels, on_device(): pl.pallas_call(early_student_kernel, out_shape=(*student_shapes, jax.Shap...  5.85 us
    pallas_call x1, Pallas kernels, on_device(): pl.pallas_call(teacher_kernel, out_shape=(jax.ShapeDtypeStruct((16 * TOK...  4.73 us
    pallas_call x1, Pallas kernels, on_device(): pl.pallas_call(grad_kernel, out_shape=jax.ShapeDtypeStruct((DS, 2 * TILE)...  3.74 us
    ppermute x1, starting transfers between devices, on_device(): recv = lax.ppermute(send, 'role', [(0, 1), (1, 0)])  1.92 us
    ppermute x1, waiting for transfers between devices, on_device(): recv = lax.ppermute(send, 'role', [(0, 1), (1, 0)])  1.57 us
  transfers between devices with their start and end apart: 1, of which 1 were waited for; matrix products, arithmetic and copies ran while one was open for 0% of the time, Pallas kernels for 2%

profile of v7, /device:TPU:8, one launch (start us, length us, event | category | flops | bytes accessed | tf_op | source)
XLA Modules:
  0.0 78.0 jit_solution(8816456163848913452)
XLA Ops:
  0.0 0.0 copy-start
  0.0 0.0 copy-start.1
  0.0 4.7 %teacher.1 = (bf16[4112,128]{1,0:T(8,128)(2,1)}, bf16[288,256,128]{2,1,0:T(8,128)(2,1)}) custom-call(s32[8,128]{1,0:T(8,128)} %bitcast.11, bf16[256,1024]{1,0:T(8,128)(2,1)} %rows_hbm.3, f32[1,1024]{1,0:T(1,128)} %bitcast.12, bf16[8,8,128,128]{3,2,1,0:T(8,128)(2,1)} %tiles_hbm.1), custom_call_target="tpu_custom_call" | custom-call | flops 540000000 | bytes 6000000 | tf_op jit(solution)/shard_map/teacher/pallas_call | solution.py:328
  4.7 1.9 %collective-permute-start = (bf16[4112,128]{1,0:T(8,128)(2,1)}, bf16[4112,128]{1,0:T(8,128)(2,1)S(1)}, u32[]{:S(2)}, u32[]{:S(2)}) collective-permute-start(bf16[4112,128]{1,0:T(8,128)(2,1)} %get-tuple-element.42), channel_id=1, source_target_pairs={{0,1},{1,0},{2,3},{3,2},{4,5},{5,4},{6,7},{7,6},{8,9},{9,8},{10,11... | collective-permute-start | bytes 3158024 | tf_op jit(solution)/shard_map/ppermute | solution.py:351
  6.7 0.0 copy-done
  6.7 0.0 copy-done.1
  6.7 1.2 %route.1 = (bf16[1056,512]{1,0:T(8,128)(2,1)S(1)}, s32[8,256]{1,0:T(8,128)S(1)}, bf16[48,256]{1,0:T(8,128)(2,1)S(1)}, bf16[16,128]{1,0:T(8,128)(2,1)S(1)}, bf16[...) custom-call(s32[1,256]{1,0:T(1,128)S(1)} %bitcast.10, f32[1,4096]{1,0:T(1,128)S(1)} %bitcast.9, ...), custom_call_target="tpu_custom_call" | custom-call | flops 100000000 | bytes 4000000 | tf_op jit(solution)/shard_map/route/pallas_call | solution.py:355
  7.9 1.6 %collective-permute-done.recv_ref = bf16[4112,128]{1,0:T(8,128)(2,1)S(1)} collective-permute-done((bf16[4112,128]{1,0:T(8,128)(2,1)}, bf16[4112,128]{1,0:T(8,128)(2,1)S(1)}, u32[]{:S(2)}, u32[]{:S(2)}) %collective-permute-start) | collective-permute-done | bytes 1052704 | tf_op jit(solution)/shard_map/ppermute | solution.py:351
  9.5 0.2 chip.1.line_ref
  9.8 5.9 %early_student.1 = (f32[480,256]{1,0:T(8,128)S(1)}, bf16[16384,480]{1,0:T(8,128)(2,1)}, bf16[512,480]{1,0:T(8,128)(2,1)S(1)}) custom-call(bf16[480,4096]{1,0:T(8,128)(2,1)} %rows_hbm.5, f32[1,4096]{1,0:T(1,128)S(1)} %get-tuple-element.43.gain_ref, bf16[4096,256]{1,0:T(8,128)(2,1)} %weight_hbm.3, bf16[4,1040,128]{2,1,0:T(8,128)(2,1)S(1)} %chip.1.line_ref), custom_call_target="tpu_custom_call" | custom-call | flops 2000000000 | bytes 10000000 | tf_op jit(solution)/shard_map/early_student/pallas_call | solution.py:395
  15.6 15.1 %all_to_all.10.recv_ref = bf16[4,1040,128]{2,1,0:T(8,128)(2,1)S(1)} all-to-all(bf16[4,1040,128]{2,1,0:T(8,128)(2,1)S(1)} %chip.1.line_ref), channel_id=1, replica_groups={{0,2,4,6},{8,10,12,14},{1,3,5,7},{9,11,13,15},{16,18,20,22},{24,26,28,3..., dimensions={0} | all-to-all | bytes 2129920 | tf_op jit(solution)/shard_map/all_to_all | solution.py:407
  30.7 0.6 pack.1
  31.3 42.8 %all_to_all.11 = bf16[96,11,2,128]{3,2,1,0:T(2,128)(2,1)S(1)} all-to-all(bf16[96,11,2,128]{3,2,1,0:T(2,128)(2,1)S(1)} %bitcast.8), channel_id=1, replica_groups={{0,16,32,48,64,80,96,112,128,144,160,176,192,208,224,240,256,272,288,30..., dimensions={0} | all-to-all | bytes 1081344 | tf_op jit(solution)/shard_map/all_to_all | solution.py:423
  74.1 0.1 late_student.1
  74.2 3.7 %grad.1 = bf16[4096,256]{1,0:T(8,128)(2,1)} custom-call(bf16[2112,128]{1,0:T(8,128)(2,1)S(1)} %bitcast.7, f32[480,256]{1,0:T(8,128)S(1)} %get-tuple-element.54.early_ref, f32[480,256]{1,0:T(8,128)S(1)} %get-tuple-element.56.late_ref, bf16[512,480]{1,0:T(8,128)(2,1)S(1)} %get-tuple-element.57.head_ref, bf16[16384,480]{1,0:T(8,128)(2,1)} %get-tuple-element.58.stash_hbm), custom_call_target="tpu_custom_call" | custom-call | flops 1000000000 | bytes 7000000 | tf_op jit(solution)/shard_map/grad/pallas_call | solution.py:444
Async XLA Ops:
  0.0 6.7 %copy-start = (f32[4096]{0:T(1024)S(1)}, f32[4096]{0:T(1024)}, u32[]{:S(2)}) copy-start(f32[4096]{0:T(1024)} %param.14) | copy-start | bytes 49156
  0.0 6.7 %copy-start.1 = (s32[256,1]{0,1:T(1,128)S(1)}, s32[256,1]{0,1:T(1,128)}, u32[]{:S(2)}) copy-start(s32[256,1]{0,1:T(1,128)} %param.12) | copy-start | bytes 3076
  4.7 4.8 %collective-permute-start = (bf16[4112,128]{1,0:T(8,128)(2,1)}, bf16[4112,128]{1,0:T(8,128)(2,1)S(1)}, u32[]{:S(2)}, u32[]{:S(2)}) collective-permute-start(bf16[4112,128]{1,0:T(8,128)(2,1)} %get-tuple-element.42), channel_id=1, source_target_pairs={{0,1},{1,0},{2,3},{3,2},{4,5},{5,4},{6,7},{7,6},{8,9},{9,8},{10,11... | collective-permute-start | bytes 3158024 | tf_op jit(solution)/shard_map/ppermute | solution.py:351
